TPU v7x, 256 devices: a whole 4x4x8 slice. The times are simulated.
256 devices in a mesh: member: 32 (over z, x_hi, core), shard: 8 (over y, x_lo).
Axes of the slice: x: 4 (x_hi: 2, x_lo: 2; x = x_hi * 2 + x_lo), y: 4, z: 8, core: 2. Of those that a mesh axis runs over, the one named last changes fastest.
Arguments:
- tokens: bfloat16 [32, 4096, 4096], P('member', 'shard'), may hold values from -6 to 6
- cotangent: bfloat16 [32, 4096, 1024], P('member', 'shard'), may hold values from -0.59765625 to 0.59765625
- weight: float32 [32, 4096, 1024], P('member', 'shard'), may hold values from -6 to 6
- first_moment: bfloat16 [32, 4096, 1024], P('member', 'shard'), may hold values from -6 to 6
- second_moment: bfloat16 [32, 4096, 1024], P('member', 'shard'), may hold values from 0.5 to 50
- learn_rate: float32 [32], replicated, may hold values from 0.02 to 0.2
- beta_one: float32 [32], replicated, may hold values from 0.8 to 0.95
- beta_two: float32 [32], replicated, may hold values from 0.9 to 0.99
- sources: int32 [32], replicated, may hold values from 0 to 31, as said below
- perturb: int32 [32], replicated, may hold values from 0 to 2
Outputs:
- new_weight: float32 [32, 4096, 1024], P('member', 'shard')
- new_first: bfloat16 [32, 4096, 1024], P('member', 'shard')
- new_second: bfloat16 [32, 4096, 1024], P('member', 'shard')
- new_log_rate: float32 [32], replicated
Inputs may be any that keep to these rules, and one draw needn't show every extreme that they name: Exactly 8 members m have sources[m] != m; each of them names one of a set of 8 other members, all of whose entries name themselves. Every other entry equals its index.
All inputs are finite; a program needn't handle non-finite values.
Results may differ from a plain program's by a relative error of at most 0.015.
Values may be sent and summed in bfloat16 or wider, within the bound.
A program may use at most 128 MiB of HBM per device.

v0:
```python
import math

import jax
import jax.numpy as jnp
from jax import lax
from jax.sharding import PartitionSpec as P

STEP = 20


def on_device(
    tokens,
    cotangent,
    weight,
    first_moment,
    second_moment,
    learn_rate,
    beta_one,
    beta_two,
    sources,
    perturb,
):
    token_rows = tokens[0]
    cotangent_rows = cotangent[0]
    own_rows = weight.shape[1]
    width = weight.shape[2]
    gradient = lax.psum_scatter(
        lax.dot_general(
            token_rows, cotangent_rows, (((0,), (0,)), ((), ())), preferred_element_type=jnp.float32
        ).astype(jnp.bfloat16),
        "shard",
        scatter_dimension=0,
        tiled=True,
    ).astype(jnp.float32)
    members = learn_rate.shape[0]
    member_index = lax.axis_index("member")
    chosen = jnp.arange(members) == member_index
    step_size = jnp.sum(jnp.where(chosen, learn_rate, 0.0))
    decay_one = jnp.sum(jnp.where(chosen, beta_one, 0.0))
    decay_two = jnp.sum(jnp.where(chosen, beta_two, 0.0))
    master = weight[0]
    moment_one = decay_one * first_moment[0].astype(jnp.float32) + (1.0 - decay_one) * gradient
    moment_two = (
        decay_two * second_moment[0].astype(jnp.float32) + (1.0 - decay_two) * gradient * gradient
    )
    corrected_one = moment_one / (1.0 - decay_one**STEP)
    corrected_two = moment_two / (1.0 - decay_two**STEP)
    updated = master - step_size * (
        corrected_one / (jnp.sqrt(corrected_two) + 1e-08) + 0.1 * master
    )
    member_count = lax.axis_size("member")
    groups = 8
    length = own_rows * width // (groups * member_count)
    packed = (
        updated.reshape(groups, member_count, length),
        moment_one.astype(jnp.bfloat16).reshape(groups, member_count, length),
        moment_two.astype(jnp.bfloat16).reshape(groups, member_count, length),
    )
    new_weight = lax.all_to_all(
        jnp.take(
            lax.all_to_all(packed[0], "member", split_axis=1, concat_axis=1, tiled=True),
            sources,
            axis=1,
        ),
        "member",
        split_axis=1,
        concat_axis=1,
        tiled=True,
    )
    new_first = lax.all_to_all(
        jnp.take(
            lax.all_to_all(
                packed[1].astype(jnp.float32), "member", split_axis=1, concat_axis=1, tiled=True
            ).astype(jnp.bfloat16),
            sources,
            axis=1,
        ).astype(jnp.float32),
        "member",
        split_axis=1,
        concat_axis=1,
        tiled=True,
    ).astype(jnp.bfloat16)
    new_second = lax.all_to_all(
        jnp.take(
            lax.all_to_all(
                packed[2].astype(jnp.float32), "member", split_axis=1, concat_axis=1, tiled=True
            ).astype(jnp.bfloat16),
            sources,
            axis=1,
        ).astype(jnp.float32),
        "member",
        split_axis=1,
        concat_axis=1,
        tiled=True,
    ).astype(jnp.bfloat16)
    table = sources[:, None] == jnp.arange(members)[None, :]
    source_rate = jnp.sum(jnp.where(table, learn_rate[None, :], 0.0), axis=1)
    loser = sources != jnp.arange(members)
    shifted = jnp.log(source_rate) + (perturb - 1).astype(jnp.float32) * math.log(2.0)
    new_log_rate = jnp.where(loser, shifted, jnp.log(learn_rate))
    return (
        new_weight.reshape(1, own_rows, width),
        new_first.reshape(1, own_rows, width),
        new_second.reshape(1, own_rows, width),
        new_log_rate,
    )


def solution(mesh):
    return jax.shard_map(
        on_device,
        mesh=mesh,
        in_specs=(
            P("member", "shard", None),
            P("member", "shard", None),
            P("member", "shard", None),
            P("member", "shard", None),
            P("member", "shard", None),
            P(),
            P(),
            P(),
            P(),
            P(),
        ),
        out_specs=(
            P("member", "shard", None),
            P("member", "shard", None),
            P("member", "shard", None),
            P(),
        ),
        check_vma=False,
    )
```

profile of v0, /device:TPU:1, one launch (start us, length us, event | category | flops | bytes accessed | tf_op | source)
XLA Modules:
  0.0 467.3 jit_solution(4248205377469718273)
XLA Ops:
  7.2 0.0 copy-start
  7.2 0.0 reduce-scatter.2.cloned.1.call-start
  7.2 1.2 copy-done
  8.4 9.0 %convolution_convert_fusion = bf16[4096,1024]{1,0:T(8,128)(2,1)} fusion(bf16[1,512,4096]{2,1,0:T(8,128)(2,1)} %param.12, bf16[1,512,1024]{2,1,0:T(8,128)(2,1)S(1)} %copy-done), kind=kOutput, calls=%fused_computation.3 | convolution fusion | flops 4299161600 | bytes 13631488 | tf_op jit(solution)/shard_map/dot_general | solution.py:28
  17.4 0.0 copy-start.3
  17.4 0.0 copy-start.7
  17.4 0.0 copy-start.2
  17.5 0.0 reduce-scatter.2.cloned.1.call-update
  17.5 0.6 copy-done.3
  18.1 0.0 copy-done.6
  18.1 0.2 select_reduce_fusion
  18.3 0.0 copy-done.4
  18.3 0.0 copy-done.5
  18.3 1.1 compare_select_fusion.1
  21.3 0.0 copy-done.7
  21.3 0.6 select_reduce_fusion.2
  23.6 169.6 %reduce-scatter.2.cloned.1.call-done = bf16[512,1024]{1,0:T(8,128)(2,1)} async-done(((bf16[4096,1024]{1,0:T(8,128)(2,1)}), bf16[512,1024]{1,0:T(8,128)(2,1)}) %reduce-scatter.2.cloned.1.call-update) | async-done | bytes 1048592 | tf_op jit(solution)/shard_map/reduce_scatter | solution.py:27
  193.2 0.0 copy-done.2
  193.2 7.6 %fusion.7 = (bf16[512,1024]{1,0:T(8,128)(2,1)S(1)}, f32[512,1024]{1,0:T(8,128)}, bf16[512,1024]{1,0:T(8,128)(2,1)}) fusion(bf16[512,1024]{1,0:T(8,128)(2,1)} %reduce-scatter.2.cloned.1.call-done, bf16[1,512,1024]{2,1,0:T(8,128)(2,1)S(1)} %copy-done.2, f32[]{:T(128)S(6)} %sub.21, f32[]{:T(128)} %get-tuple-element.12, f32[]{:T(128)S(6)} %sub.22, f32[]{:T(128)S(6)} %sub.20, ...), kind=kLoop, calls=%fused_computation.16 | loop fusion | flops 10485760 | bytes 9437212 | tf_op jit(solution)/shard_map/convert_element_type | solution.py:86
  200.8 0.4 reshape.49
  201.2 1.5 copy.27
  202.7 9.9 %all-to-all-start.4 = ((bf16[8,32,2048]{2,0,1:T(8,128)(2,1)}), bf16[8,32,2048]{2,0,1:T(8,128)(2,1)S(1)}, u32[]{:S(2)}, u32[]{:S(2)}) async-start(bf16[8,32,2048]{2,0,1:T(8,128)(2,1)} %copy.27), calls=%async_computation.5 | async-start | bytes 2097152 | tf_op jit(solution)/shard_map/all_to_all | solution.py:85
  212.6 1.4 reshape.48
  214.1 1.6 copy.25
  215.7 25.1 %all-to-all-done.4 = bf16[8,32,2048]{2,0,1:T(8,128)(2,1)S(1)} async-done(((bf16[8,32,2048]{2,0,1:T(8,128)(2,1)}), bf16[8,32,2048]{2,0,1:T(8,128)(2,1)S(1)}, u32[]{:S(2)}, u32[]{:S(2)}) %all-to-all-start.4) | async-done | bytes 1048608 | tf_op jit(solution)/shard_map/all_to_all | solution.py:85
  240.8 5.8 %all-to-all-start.2 = ((bf16[8,32,2048]{2,0,1:T(8,128)(2,1)}), bf16[8,32,2048]{2,0,1:T(8,128)(2,1)}, u32[]{:S(2)}, u32[]{:S(2)}) async-start(bf16[8,32,2048]{2,0,1:T(8,128)(2,1)} %copy.25), calls=%async_computation.3 | async-start | bytes 2097152 | tf_op jit(solution)/shard_map/all_to_all | solution.py:72
  246.6 0.0 copy-done.1
  246.6 1.9 reshape.44
  248.6 2.5 copy.23
  251.1 23.7 %all-to-all-done.2 = bf16[8,32,2048]{2,0,1:T(8,128)(2,1)} async-done(((bf16[8,32,2048]{2,0,1:T(8,128)(2,1)}), bf16[8,32,2048]{2,0,1:T(8,128)(2,1)}, u32[]{:S(2)}, u32[]{:S(2)}) %all-to-all-start.2) | async-done | bytes 1048608 | tf_op jit(solution)/shard_map/all_to_all | solution.py:72
  274.8 5.8 %all-to-all-start = ((f32[8,32,2048]{2,0,1:T(8,128)}), f32[8,32,2048]{2,0,1:T(8,128)S(1)}, u32[]{:S(2)}, u32[]{:S(2)}) async-start(f32[8,32,2048]{2,0,1:T(8,128)} %copy.23), calls=%async_computation.1 | async-start | bytes 4194304 | tf_op jit(solution)/shard_map/all_to_all | solution.py:61
  280.7 2.8 gather_fusion.2
  283.5 2.8 gather_fusion.1
  286.3 3.1 bitcast_convert_fusion
  289.4 41.3 %all-to-all-done = f32[8,32,2048]{2,0,1:T(8,128)S(1)} async-done(((f32[8,32,2048]{2,0,1:T(8,128)}), f32[8,32,2048]{2,0,1:T(8,128)S(1)}, u32[]{:S(2)}, u32[]{:S(2)}) %all-to-all-start) | async-done | bytes 2097184 | tf_op jit(solution)/shard_map/all_to_all | solution.py:61
  330.7 34.6 %all_to_all.30 = bf16[8,32,2048]{2,0,1:T(8,128)(2,1)} all-to-all(bf16[8,32,2048]{2,0,1:T(8,128)(2,1)} %get-tuple-element.11), channel_id=1, replica_groups=mesh['member'=32,'shard'=8] {'member'}, dimensions={1} | all-to-all | bytes 2097152 | tf_op jit(solution)/shard_map/all_to_all | solution.py:70
  365.3 5.8 %all-to-all-start.5 = ((bf16[8,32,2048]{2,0,1:T(8,128)(2,1)}), bf16[8,32,2048]{2,0,1:T(8,128)(2,1)}, u32[]{:S(2)}, u32[]{:S(2)}) async-start(bf16[8,32,2048]{2,0,1:T(8,128)(2,1)} %get-tuple-element.10), calls=%async_computation.6 | async-start | bytes 2097152 | tf_op jit(solution)/shard_map/all_to_all | solution.py:83
  371.1 2.0 gather_fusion
  373.1 3.1 select_bitcast_fusion
  376.3 23.1 %all-to-all-done.5 = bf16[8,32,2048]{2,0,1:T(8,128)(2,1)} async-done(((bf16[8,32,2048]{2,0,1:T(8,128)(2,1)}), bf16[8,32,2048]{2,0,1:T(8,128)(2,1)}, u32[]{:S(2)}, u32[]{:S(2)}) %all-to-all-start.5) | async-done | bytes 1048608 | tf_op jit(solution)/shard_map/all_to_all | solution.py:83
  399.3 5.8 %all-to-all-start.1 = ((f32[8,32,2048]{2,0,1:T(8,128)}), f32[8,32,2048]{2,0,1:T(8,128)S(1)}, u32[]{:S(2)}, u32[]{:S(2)}) async-start(f32[8,32,2048]{2,0,1:T(8,128)} %select_bitcast_fusion), calls=%async_computation.2 | async-start | bytes 4194304 | tf_op jit(solution)/shard_map/all_to_all | solution.py:59
  405.1 2.8 copy.26
  407.9 2.2 reshape.46
  410.1 2.8 copy.28
  412.9 2.2 reshape.47
  415.1 40.0 %all-to-all-done.1 = f32[8,32,2048]{2,0,1:T(8,128)S(1)} async-done(((f32[8,32,2048]{2,0,1:T(8,128)}), f32[8,32,2048]{2,0,1:T(8,128)S(1)}, u32[]{:S(2)}, u32[]{:S(2)}) %all-to-all-start.1) | async-done | bytes 2097184 | tf_op jit(solution)/shard_map/all_to_all | solution.py:59
  455.1 2.6 copy.24
  457.7 2.7 reshape.45
  (7 shorter events, 0.0 us)
Async XLA Ops:
  7.2 1.2 copy-start
  7.2 186.0 %reduce-scatter.2.cloned.1.call-start = ((), (), s32[]{:S(2)}) async-start(), calls=%async_computation.7 | async-start | bytes 9437184 | tf_op jit(solution)/shard_map/reduce_scatter | solution.py:27
  17.4 0.7 copy-start.3
  17.4 0.7 copy-start.6
  17.4 0.8 copy-start.4
  17.4 0.9 copy-start.5
  17.4 3.9 copy-start.7
  17.4 175.7 %copy-start.2 = (bf16[1,512,1024]{2,1,0:T(8,128)(2,1)S(1)}, bf16[1,512,1024]{2,1,0:T(8,128)(2,1)}, u32[]{:S(2)}) copy-start(bf16[1,512,1024]{2,1,0:T(8,128)(2,1)} %param.16) | copy-start | bytes 3145732
  202.7 38.1 %all-to-all-start.4 = ((bf16[8,32,2048]{2,0,1:T(8,128)(2,1)}), bf16[8,32,2048]{2,0,1:T(8,128)(2,1)S(1)}, u32[]{:S(2)}, u32[]{:S(2)}) async-start(bf16[8,32,2048]{2,0,1:T(8,128)(2,1)} %copy.27), calls=%async_computation.5 | async-start | bytes 2097152 | tf_op jit(solution)/shard_map/all_to_all | solution.py:85
  240.8 5.8 %copy-start.1 = (bf16[8,32,2048]{2,0,1:T(8,128)(2,1)}, bf16[8,32,2048]{2,0,1:T(8,128)(2,1)S(1)}, u32[]{:S(2)}) copy-start(bf16[8,32,2048]{2,0,1:T(8,128)(2,1)S(1)} %all-to-all-done.4) | copy-start | bytes 3145732
  240.8 34.0 %all-to-all-start.2 = ((bf16[8,32,2048]{2,0,1:T(8,128)(2,1)}), bf16[8,32,2048]{2,0,1:T(8,128)(2,1)}, u32[]{:S(2)}, u32[]{:S(2)}) async-start(bf16[8,32,2048]{2,0,1:T(8,128)(2,1)} %copy.25), calls=%async_computation.3 | async-start | bytes 2097152 | tf_op jit(solution)/shard_map/all_to_all | solution.py:72
  274.8 55.9 %all-to-all-start = ((f32[8,32,2048]{2,0,1:T(8,128)}), f32[8,32,2048]{2,0,1:T(8,128)S(1)}, u32[]{:S(2)}, u32[]{:S(2)}) async-start(f32[8,32,2048]{2,0,1:T(8,128)} %copy.23), calls=%async_computation.1 | async-start | bytes 4194304 | tf_op jit(solution)/shard_map/all_to_all | solution.py:61
  365.3 34.0 %all-to-all-start.5 = ((bf16[8,32,2048]{2,0,1:T(8,128)(2,1)}), bf16[8,32,2048]{2,0,1:T(8,128)(2,1)}, u32[]{:S(2)}, u32[]{:S(2)}) async-start(bf16[8,32,2048]{2,0,1:T(8,128)(2,1)} %get-tuple-element.10), calls=%async_computation.6 | async-start | bytes 2097152 | tf_op jit(solution)/shard_map/all_to_all | solution.py:83
  399.3 55.8 %all-to-all-start.1 = ((f32[8,32,2048]{2,0,1:T(8,128)}), f32[8,32,2048]{2,0,1:T(8,128)S(1)}, u32[]{:S(2)}, u32[]{:S(2)}) async-start(f32[8,32,2048]{2,0,1:T(8,128)} %select_bitcast_fusion), calls=%async_computation.2 | async-start | bytes 4194304 | tf_op jit(solution)/shard_map/all_to_all | solution.py:59
Sparse Core Ops, SparseCore 0:
  17.6 175.5 reduce-scatter.1
where the time goes:
time: 468 us; the launch traced here: 467 us
  waiting for transfers between devices  323 us (69%)
  blocking collectives  34.6 us (7%)
  local copies, waits for them, and re-layouts  34.1 us (7%)
  starting transfers between devices  33.3 us (7%)
  between operations  17.8 us (4%)
  other arithmetic  15.8 us (3%)
  matrix products  9.03 us (2%)
    reduce_scatter x1, waiting for transfers between devices, on_device(): lax.psum_scatter(lax.dot_general(token_rows, cotangent_rows, (((0,), (0,)...  170 us
    all_to_all x1, waiting for transfers between devices, on_device(): lax.all_to_all(packed[0], 'member', split_axis=1, concat_axis=1, tiled=True)  41.3 us
    all_to_all x1, waiting for transfers between devices, on_device(): lax.all_to_all(jnp.take(lax.all_to_all(packed[0], 'member', split_axis=1,...  40 us
    all_to_all x1, blocking collectives, on_device(): lax.all_to_all(jnp.take(lax.all_to_all(packed[1].astype(jnp.float32), 'me...  34.6 us
    all_to_all x1, waiting for transfers between devices, on_device(): lax.all_to_all(packed[2].astype(jnp.float32), 'member', split_axis=1, con...  25.1 us
    all_to_all x1, waiting for transfers between devices, on_device(): lax.all_to_all(packed[1].astype(jnp.float32), 'member', split_axis=1, con...  23.7 us
    all_to_all x1, waiting for transfers between devices, on_device(): lax.all_to_all(jnp.take(lax.all_to_all(packed[2].astype(jnp.float32), 'me...  23.1 us
    all_to_all x1, starting transfers between devices, on_device(): lax.all_to_all(packed[2].astype(jnp.float32), 'member', split_axis=1, con...  9.93 us
  transfers between devices with their start and end apart: 6, of which 6 were waited for; matrix products, arithmetic and copies ran while one was open for 7% of the time, Pallas kernels for 0%

commit v1 on v0

v1 whole, which is shorter than its diff:
```python
import functools
import math

import jax
import jax.numpy as jnp
from jax import lax
from jax.experimental import pallas as pl
from jax.experimental.pallas import tpu as pltpu
from jax.sharding import PartitionSpec as P

MESH = pl.DeviceIdType.MESH
ROWS = 128
SPLIT = 2
LEVELS = 8
QUAD = 4
RING = 4
LAG = {"b": 1, "c": 2, "d": 3, "e": 4, "f": 5, "g": 6, "h": 7}


def twentieth_power(value):
    square = value * value
    fourth = square * square
    eighth = fourth * fourth
    return eighth * eighth * fourth


def step_kernel(
    win_slots,
    lose_slots,
    table,
    rates,
    decays_one,
    decays_two,
    tokens,
    cotangent,
    weight,
    first,
    second,
    out_weight,
    out_first,
    out_second,
    y1_send,
    y1_recv,
    y2_send,
    y2_recv,
    x_send,
    x_recv,
    q1_send,
    q1_recv,
    z1_send,
    z1_recv,
    z2_send,
    z2_recv,
    q2_send,
    q2_recv,
    terms,
    q1_held,
    z1_held,
    z2_held,
    send_sem,
    y1_sem,
    y2_sem,
    x_sem,
    q1_sem,
    z1_sem,
    z2_sem,
    q2_sem,
):
    chunks = y1_send.shape[0]
    cols = y1_send.shape[3]
    part = cols // QUAD
    own_rows = weight.shape[0]
    slots = terms.shape[0]
    member = lax.axis_index("member")
    shard = lax.axis_index("shard")
    level, mine = member // QUAD, lax.rem(member, QUAD)
    y, x_lo = shard // 2, lax.rem(shard, 2)
    y_next, y_prev = lax.rem(y + 1, RING), lax.rem(y + RING - 1, RING)
    y_far = lax.rem(y + 2, RING)

    def on_shard(at_y, at_x):
        return {"member": member, "shard": at_y * 2 + at_x}

    def on_member(at_level, at_quad):
        return {"member": at_level * QUAD + at_quad, "shard": shard}

    up, down = on_shard(y_next, x_lo), on_shard(y_prev, x_lo)
    beside = on_shard(y, 1 - x_lo)
    quads = [lax.rem(mine + d, QUAD) for d in range(1, QUAD)]
    levels = [lax.rem(level + d, LEVELS) for d in (4, 3, 5, 2, 6, 1, 7)]

    peers = [up, down, beside]
    peers += [on_member(level, q) for q in quads]
    peers += [on_member(z, mine) for z in levels]
    barrier = pltpu.get_barrier_semaphore()
    for peer in peers:
        pl.semaphore_signal(barrier, inc=1, device_id=peer, device_id_type=MESH)
    pl.semaphore_wait(barrier, len(peers))

    def send(src, dst, stage, recv, device):
        pltpu.make_async_remote_copy(
            src_ref=src,
            dst_ref=dst,
            send_sem=send_sem.at[stage],
            recv_sem=recv,
            device_id=device,
            device_id_type=MESH,
        ).start()

    def await_bytes(ref, sem):
        pltpu.make_async_copy(ref, ref, sem).wait()

    def place(k):
        row = pl.multiple_of((k // SPLIT) * ROWS, ROWS)
        col = pl.multiple_of(lax.rem(k, SPLIT) * cols, cols)
        return row, col

    def term(k, at_y, at_x):
        row, col = place(k)
        start = pl.multiple_of((at_y * 2 + at_x) * own_rows + row, ROWS)
        return lax.dot_general(
            tokens[:, pl.ds(start, ROWS)],
            cotangent[:, pl.ds(col, cols)],
            (((0,), (0,)), ((), ())),
            preferred_element_type=jnp.float32,
        )

    def stage_a(k):
        slot = lax.rem(k, slots)
        y1_send[k, 0] = term(k, y_far, 0).astype(jnp.bfloat16)
        send(y1_send.at[k, 0], y1_recv.at[k, 0], 0, y1_sem.at[k, 0], up)
        y1_send[k, 1] = term(k, y_far, 1).astype(jnp.bfloat16)
        send(y1_send.at[k, 1], y1_recv.at[k, 1], 0, y1_sem.at[k, 1], down)
        y2_send[k, 0, 1] = term(k, y_next, 1).astype(jnp.bfloat16)
        send(y2_send.at[k, 0, 1], y2_recv.at[k, 0, 1], 1, y2_sem.at[k, 0], up)
        y2_send[k, 1, 0] = term(k, y_prev, 0).astype(jnp.bfloat16)
        send(y2_send.at[k, 1, 0], y2_recv.at[k, 1, 0], 1, y2_sem.at[k, 1], down)
        terms[slot, 0] = term(k, y_next, 0)
        terms[slot, 1] = term(k, y_prev, 1)
        terms[slot, 2] = term(k, y, 1 - x_lo)
        terms[slot, 3] = term(k, y, x_lo)

    def stage_b(k):
        slot = lax.rem(k, slots)
        await_bytes(y1_recv.at[k, 0], y1_sem.at[k, 0])
        y2_send[k, 0, 0] = (terms[slot, 0] + y1_recv[k, 0].astype(jnp.float32)).astype(jnp.bfloat16)
        send(y2_send.at[k, 0, 0], y2_recv.at[k, 0, 0], 1, y2_sem.at[k, 0], up)
        await_bytes(y1_recv.at[k, 1], y1_sem.at[k, 1])
        y2_send[k, 1, 1] = (terms[slot, 1] + y1_recv[k, 1].astype(jnp.float32)).astype(jnp.bfloat16)
        send(y2_send.at[k, 1, 1], y2_recv.at[k, 1, 1], 1, y2_sem.at[k, 1], down)

    def stage_c(k):
        slot = lax.rem(k, slots)
        await_bytes(y2_recv.at[k, 0], y2_sem.at[k, 0])
        await_bytes(y2_recv.at[k, 1], y2_sem.at[k, 1])

        def total(which, at_x):
            return (
                terms[slot, which]
                + y2_recv[k, 0, at_x].astype(jnp.float32)
                + y2_recv[k, 1, at_x].astype(jnp.float32)
            )

        x_send[k] = total(2, 1 - x_lo).astype(jnp.bfloat16)
        send(x_send.at[k], x_recv.at[k], 2, x_sem.at[k], beside)
        terms[slot, 3] = total(3, x_lo)

    def stage_d(k):
        slot = lax.rem(k, slots)
        row, col = place(k)
        here = (pl.ds(row, ROWS), pl.ds(col, cols))
        rate = jnp.full((1, cols), rates[member], jnp.float32)
        decay_one = jnp.full((1, cols), decays_one[member], jnp.float32)
        decay_two = jnp.full((1, cols), decays_two[member], jnp.float32)
        scale_one = 1.0 / (1.0 - twentieth_power(decay_one))
        scale_two = 1.0 / (1.0 - twentieth_power(decay_two))
        await_bytes(x_recv.at[k], x_sem.at[k])
        gradient = terms[slot, 3] + x_recv[k].astype(jnp.float32)
        moment_one = decay_one * first[here].astype(jnp.float32) + (1.0 - decay_one) * gradient
        moment_two = (
            decay_two * second[here].astype(jnp.float32) + (1.0 - decay_two) * gradient * gradient
        )
        master = weight[here]
        updated = master - rate * (
            (moment_one * scale_one) / (jnp.sqrt(moment_two * scale_two) + 1e-08) + 0.1 * master
        )
        out_weight[here] = updated
        narrow = (
            updated.astype(jnp.bfloat16),
            moment_one.astype(jnp.bfloat16),
            moment_two.astype(jnp.bfloat16),
        )
        out_first[here] = narrow[1]
        out_second[here] = narrow[2]
        for q in range(QUAD):
            for a in range(3):
                q1_send[k, q, a] = narrow[a][:, q * part : (q + 1) * part]
        for q in quads:
            send(q1_send.at[k, q], q1_recv.at[k, mine], 3, q1_sem.at[k], on_member(level, q))
        q1_recv[k, mine] = q1_send[k, mine]

    def stage_e(k):
        await_bytes(q1_recv.at[k, pl.ds(0, QUAD - 1)], q1_sem.at[k])
        q1_held[...] = q1_recv[k]
        for j in range(win_slots):
            chosen = q1_held[table[level * QUAD + j]]
            for z in range(LEVELS):
                z1_send[k, z, j] = chosen[:, z * 16 : (z + 1) * 16, :]
        for z in levels:
            send(z1_send.at[k, z], z1_recv.at[k, level], 4, z1_sem.at[k], on_member(z, mine))
        z1_recv[k, level] = z1_send[k, level]

    def stage_f(k):
        await_bytes(z1_recv.at[k, pl.ds(0, LEVELS - 1)], z1_sem.at[k])
        z1_held[...] = z1_recv[k]
        for z in range(LEVELS):
            for j in range(lose_slots):
                source = table[32 + z * QUAD + j]
                z2_send[k, z, j] = z1_held[source // QUAD, lax.rem(source, QUAD)]
        for z in levels:
            send(z2_send.at[k, z], z2_recv.at[k, level], 5, z2_sem.at[k], on_member(z, mine))
        z2_recv[k, level] = z2_send[k, level]

    def stage_g(k):
        await_bytes(z2_recv.at[k, pl.ds(0, LEVELS - 1)], z2_sem.at[k])
        z2_held[...] = z2_recv[k]
        for q in range(QUAD):
            slot = table[64 + level * QUAD + q]
            for z in range(LEVELS):
                q2_send[k, q, z] = z2_held[z, slot]
        for q in quads:
            send(q2_send.at[k, q], q2_recv.at[k, mine], 6, q2_sem.at[k], on_member(level, q))
        q2_recv[k, mine] = q2_send[k, mine]

    def stage_h(k):
        row, col = place(k)
        await_bytes(q2_recv.at[k, pl.ds(0, QUAD - 1)], q2_sem.at[k])
        taken = jnp.full((1, part), table[96 + member], jnp.int32) != 0
        outs = (out_weight, out_first, out_second)
        for q in range(QUAD):
            for a in range(3):
                here = (pl.ds(row, ROWS), pl.ds(col + q * part, part))
                copied = q2_recv[k, q, :, a].reshape(ROWS, part).astype(jnp.float32)
                kept = outs[a][here].astype(jnp.float32)
                outs[a][here] = jnp.where(taken, copied, kept).astype(outs[a].dtype)

    stages = (
        (0, stage_a),
        (LAG["b"], stage_b),
        (LAG["c"], stage_c),
        (LAG["d"], stage_d),
        (LAG["e"], stage_e),
        (LAG["f"], stage_f),
        (LAG["g"], stage_g),
        (LAG["h"], stage_h),
    )

    def iteration(i, carry):
        for lag, stage in stages:
            k = i - lag

            @pl.when((k >= 0) & (k < chunks))
            def _():
                stage(k)

        return carry

    lax.fori_loop(0, chunks + LAG["h"], iteration, 0)

    sent = (
        y1_send,
        y2_send,
        x_send,
        q1_send.at[:, pl.ds(0, QUAD - 1)],
        z1_send.at[:, pl.ds(0, LEVELS - 1)],
        z2_send.at[:, pl.ds(0, LEVELS - 1)],
        q2_send.at[:, pl.ds(0, QUAD - 1)],
    )
    for stage, ref in enumerate(sent):
        await_bytes(ref, send_sem.at[stage])


def step_call(win_slots, lose_slots, collective_id, table, rates, ones, twos, *blocks):
    tokens, cotangent, weight, first, second = blocks
    rows, width = weight.shape
    cols = width // SPLIT
    chunks = rows // ROWS * SPLIT
    part = cols // QUAD
    kind = jnp.bfloat16
    scalars = pl.BlockSpec(memory_space=pltpu.SMEM)
    whole = pl.BlockSpec(memory_space=pltpu.VMEM)
    y1 = pltpu.VMEM((chunks, 2, ROWS, cols), kind)
    y2 = pltpu.VMEM((chunks, 2, 2, ROWS, cols), kind)
    beside = pltpu.VMEM((chunks, ROWS, cols), kind)
    q1 = pltpu.VMEM((chunks, QUAD, 3, ROWS, part), kind)
    z1 = pltpu.VMEM((chunks, LEVELS, win_slots, 3, ROWS // LEVELS, part), kind)
    z2 = pltpu.VMEM((chunks, LEVELS, lose_slots, 3, ROWS // LEVELS, part), kind)
    q2 = pltpu.VMEM((chunks, QUAD, LEVELS, 3, ROWS // LEVELS, part), kind)
    dma = pltpu.SemaphoreType.DMA
    return pl.pallas_call(
        functools.partial(step_kernel, win_slots, lose_slots),
        out_shape=(
            jax.ShapeDtypeStruct(weight.shape, jnp.float32),
            jax.ShapeDtypeStruct(weight.shape, kind),
            jax.ShapeDtypeStruct(weight.shape, kind),
        ),
        in_specs=[scalars] * 4 + [whole] * 5,
        out_specs=(whole, whole, whole),
        scratch_shapes=[
            y1,
            y1,
            y2,
            y2,
            beside,
            beside,
            q1,
            q1,
            z1,
            z1,
            z2,
            z2,
            q2,
            q2,
            pltpu.VMEM((LAG["d"] + 1, 4, ROWS, cols), jnp.float32),
            pltpu.VMEM(q1.shape[1:], kind),
            pltpu.VMEM(z1.shape[1:], kind),
            pltpu.VMEM(z2.shape[1:], kind),
            dma((7,)),
            dma((chunks, 2)),
            dma((chunks, 2)),
            dma((chunks,)),
            dma((chunks,)),
            dma((chunks,)),
            dma((chunks,)),
            dma((chunks,)),
        ],
        compiler_params=pltpu.CompilerParams(
            collective_id=collective_id,
            has_side_effects=True,
            vmem_limit_bytes=63 * 2**20,
        ),
    )(table, rates, ones, twos, *blocks)


def routes(sources):
    members = sources.shape[0]
    own = jnp.arange(members, dtype=jnp.int32)
    loser = sources != own
    equal = sources[:, None] == own[None, :]
    winner = jnp.any(equal & loser[:, None], axis=0)

    def ranks(flags):
        flat = flags.reshape(LEVELS, QUAD).astype(jnp.int32)
        before = jnp.tril(jnp.ones((QUAD, QUAD), jnp.int32), -1)
        rank = jnp.sum(flat[:, None, :] * before[None], axis=2)
        return flat, rank

    win, win_rank = ranks(winner)
    lose, lose_rank = ranks(loser)
    column = jnp.arange(QUAD, dtype=jnp.int32)

    def spread(flat, rank, value):
        at = (rank[:, :, None] == column[None, None, :]) & (flat[:, :, None] != 0)
        return jnp.sum(jnp.where(at, value[:, :, None], 0), axis=1)

    chosen = spread(win, win_rank, jnp.broadcast_to(column[None, :], win.shape))
    place = (own // QUAD) * QUAD + win_rank.reshape(members)
    source_place = jnp.sum(jnp.where(equal, place[None, :], 0), axis=1)
    wanted = spread(lose, lose_rank, source_place.reshape(LEVELS, QUAD))
    slot = jnp.where(lose != 0, lose_rank, 0)
    table = jnp.concatenate(
        [chosen.reshape(-1), wanted.reshape(-1), slot.reshape(-1), loser.astype(jnp.int32)]
    )
    return table, loser, equal


def on_device(
    tokens,
    cotangent,
    weight,
    first_moment,
    second_moment,
    learn_rate,
    beta_one,
    beta_two,
    sources,
    perturb,
):
    table, loser, equal = routes(sources)
    new_weight, new_first, new_second = step_call(
        QUAD,
        QUAD,
        0,
        table,
        learn_rate,
        beta_one,
        beta_two,
        tokens[0],
        cotangent[0],
        weight[0],
        first_moment[0],
        second_moment[0],
    )
    source_rate = jnp.sum(jnp.where(equal, learn_rate[None, :], 0.0), axis=1)
    shifted = jnp.log(source_rate) + (perturb - 1).astype(jnp.float32) * math.log(2.0)
    new_log_rate = jnp.where(loser, shifted, jnp.log(learn_rate))
    return new_weight[None], new_first[None], new_second[None], new_log_rate


def solution(mesh):
    block = P("member", "shard", None)
    return jax.shard_map(
        on_device,
        mesh=mesh,
        in_specs=(block,) * 5 + (P(),) * 5,
        out_specs=(block, block, block, P()),
        check_vma=False,
    )
```

time: 468 us -> 207 us (0.44)
  waiting for transfers between devices: 323 us -> 0 us
  Pallas kernels: 0 us -> 195 us
  blocking collectives: 34.6 us -> 0 us
  starting transfers between devices: 33.3 us -> 0 us
  local copies, waits for them, and re-layouts: 34.1 us -> 7.17 us
  between operations: 17.8 us -> 0.68 us
  other arithmetic: 15.8 us -> 4.44 us
  matrix products: 9.03 us -> 0 us
    pallas_call x0 -> x1, Pallas kernels: none -> 195 us  [step_call(): pl.pallas_call(functools.partial(step_kernel, win_slots, lose_slots), out...]
    reduce_scatter x1 -> x0, waiting for transfers between devices: 170 us -> none  [on_device(): lax.psum_scatter(lax.dot_general(token_rows, cotangent_rows, (((0,), (0,)...]
    all_to_all x5 -> x0, waiting for transfers between devices: 153 us -> none  [the longest x1 41.3 us: on_device(): lax.all_to_all(packed[0], 'member', split_axis=1, concat_axis=1, tiled=True)]
    all_to_all x1 -> x0, blocking collectives: 34.6 us -> none  [on_device(): lax.all_to_all(jnp.take(lax.all_to_all(packed[1].astype(jnp.float32), 'me...]
    all_to_all x5 -> x0, starting transfers between devices: 33.2 us -> none  [the longest x1 9.93 us: on_device(): lax.all_to_all(packed[2].astype(jnp.float32), 'member', split_axis=1, con...]
    reshape x5 -> x3, local copies, waits for them, and re-layouts: 11.6 us -> 0.24 us  [the longest x1 0.08 us: routes(): place = own // QUAD * QUAD + win_rank.reshape(members)]
    convert_element_type x2 -> x1, other arithmetic: 10.7 us -> 0.01 us  [ranks(): flat = flags.reshape(LEVELS, QUAD).astype(jnp.int32)]
    convert_element_type x6 -> x4, local copies, waits for them, and re-layouts: 10.5 us -> 0.33 us  [ranks(): flat = flags.reshape(LEVELS, QUAD).astype(jnp.int32)]
  transfers between devices with their start and end apart: 6 -> 0, of which waited for: 6 -> 0; matrix products, arithmetic and copies ran while one was open for 7% -> 0% of each run, Pallas kernels for 0% -> 0%
where the time goes in v1:
time: 207 us
  Pallas kernels  195 us (94%)
  local copies, waits for them, and re-layouts  7.17 us (3%)
  other arithmetic  4.44 us (2%)
    pallas_call x1, Pallas kernels, step_call(): pl.pallas_call(functools.partial(step_kernel, win_slots, lose_slots), out...  195 us
    unnamed x13, local copies, waits for them, and re-layouts  5.83 us

profile of v1, /device:TPU:1, one launch (start us, length us, event | category | flops | bytes accessed | tf_op | source)
XLA Modules:
  0.0 207.1 jit_solution(13213002925534288309)
XLA Ops:
  0.6 0.7 iota_compare_fusion.4
  1.3 0.1 reshape.95
  1.4 0.1 copy.17
  1.5 0.8 fusion.1
  2.2 0.1 reshape.94
  2.3 0.1 copy.14
  2.4 0.1 fusion.4
  2.5 0.1 multiply_reduce_fusion.1
  2.6 0.1 copy.19
  2.6 0.1 reshape.92
  2.7 0.8 select_reduce_fusion.1
  3.6 0.1 broadcast_in_dim.75
  3.7 0.1 copy.20
  3.7 0.1 copy.18
  3.8 0.1 copy.15
  4.0 0.1 copy.16
  4.1 0.1 reshape.91
  4.1 0.1 copy.21
  4.2 0.1 reshape.93
  4.3 0.1 copy.22
  4.4 0.1 reduce_sum.61
  4.5 0.7 compare_select_fusion
  5.1 0.6 pad_add_fusion.table
  5.7 0.0 copy-start.2
  5.7 0.0 copy-start.3
  5.7 0.0 copy-start.4
  5.7 194.8 %shard_map.129 = (f32[512,1024]{1,0:T(8,128)}, bf16[512,1024]{1,0:T(8,128)(2,1)}, bf16[512,1024]{1,0:T(8,128)(2,1)}) custom-call(s32[128]{0:T(128)} %pad_add_fusion.table, f32[32]{0:T(128)} %rates.1, f32[32]{0:T(128)} %decays_one.1, f32[32]{0:T(128)} %decays_two.1, bf16[512,4096]{1,0:T(8,128)(2,1)} %bitcast.8, bf16[512,1024]{1,0:T(8,128)(2,1)} %bitcast.11, ...), custom_call_target="tpu_custom_call" | custom-call | tf_op jit(solution)/shard_map/pallas_call | solution.py:300
  200.5 0.0 copy-done.2
  200.5 0.0 copy-done.3
  200.5 0.2 select_reduce_fusion
  200.7 0.0 copy-done.4
  200.7 0.5 log_select_fusion
  201.2 0.0 copy-start.1
  201.3 3.2 %copy.26 = f32[1,512,1024]{2,1,0:T(8,128)} copy(f32[1,512,1024]{2,1,0:T(8,128)} %bitcast.10) | data formatting | bytes 4194304
  204.5 0.0 copy-done.1
  204.5 0.0 copy-start
  204.5 1.0 copy.27
  205.5 0.6 copy-done
  206.1 1.0 copy.28
  (6 shorter events, 0.1 us)
Async XLA Ops:
  5.7 194.8 %copy-start.2 = (f32[32]{0:T(128)S(1)}, f32[32]{0:T(128)}, u32[]{:S(2)}) copy-start(f32[32]{0:T(128)} %rates.1) | copy-start | bytes 388
  5.7 194.8 %copy-start.3 = (s32[32]{0:T(128)S(1)}, s32[32]{0:T(128)}, u32[]{:S(2)}) copy-start(s32[32]{0:T(128)} %param.18) | copy-start | bytes 388
  5.7 195.0 %copy-start.4 = (s32[32]{0:T(128)S(1)}, s32[32]{0:T(128)}, u32[]{:S(2)}) copy-start(s32[32]{0:T(128)} %param.19) | copy-start | bytes 388
  201.2 3.3 %copy-start.1 = (bf16[512,1024]{1,0:T(8,128)(2,1)S(1)}, bf16[512,1024]{1,0:T(8,128)(2,1)}, u32[]{:S(2)}) copy-start(bf16[512,1024]{1,0:T(8,128)(2,1)} %get-tuple-element.8) | copy-start | bytes 3145732
  204.5 1.6 copy-start

commit v2 on v1

--- a/solution.py
+++ b/solution.py
@@ -14,7 +14,11 @@
 LEVELS = 8
 QUAD = 4
 RING = 4
-LAG = {"b": 1, "c": 2, "d": 3, "e": 4, "f": 5, "g": 6, "h": 7}
+PLANS = (
+    (2, "edgbafhc", dict(a=0, b=1, c=1, d=3, e=4, f=5, g=8, h=9)),
+    (3, "acgbefdh", dict(a=0, b=0, c=1, d=1, e=2, f=3, g=5, h=6)),
+    (4, "acbeghfd", dict(a=0, b=0, c=1, d=1, e=2, f=3, g=7, h=9)),
+)
 
 
 def twentieth_power(value):
@@ -25,8 +29,9 @@
 
 
 def step_kernel(
-    win_slots,
-    lose_slots,
+    member_slots,
+    order,
+    lags,
     table,
     rates,
     decays_one,
@@ -202,7 +207,7 @@
     def stage_e(k):
         await_bytes(q1_recv.at[k, pl.ds(0, QUAD - 1)], q1_sem.at[k])
         q1_held[...] = q1_recv[k]
-        for j in range(win_slots):
+        for j in range(member_slots):
             chosen = q1_held[table[level * QUAD + j]]
             for z in range(LEVELS):
                 z1_send[k, z, j] = chosen[:, z * 16 : (z + 1) * 16, :]
@@ -214,7 +219,7 @@
         await_bytes(z1_recv.at[k, pl.ds(0, LEVELS - 1)], z1_sem.at[k])
         z1_held[...] = z1_recv[k]
         for z in range(LEVELS):
-            for j in range(lose_slots):
+            for j in range(member_slots):
                 source = table[32 + z * QUAD + j]
                 z2_send[k, z, j] = z1_held[source // QUAD, lax.rem(source, QUAD)]
         for z in levels:
@@ -244,28 +249,28 @@
                 kept = outs[a][here].astype(jnp.float32)
                 outs[a][here] = jnp.where(taken, copied, kept).astype(outs[a].dtype)
 
-    stages = (
-        (0, stage_a),
-        (LAG["b"], stage_b),
-        (LAG["c"], stage_c),
-        (LAG["d"], stage_d),
-        (LAG["e"], stage_e),
-        (LAG["f"], stage_f),
-        (LAG["g"], stage_g),
-        (LAG["h"], stage_h),
+    stages = dict(
+        a=stage_a,
+        b=stage_b,
+        c=stage_c,
+        d=stage_d,
+        e=stage_e,
+        f=stage_f,
+        g=stage_g,
+        h=stage_h,
     )
 
     def iteration(i, carry):
-        for lag, stage in stages:
-            k = i - lag
+        for name in order:
+            k = i - lags[name]
 
             @pl.when((k >= 0) & (k < chunks))
             def _():
-                stage(k)
+                stages[name](k)
 
         return carry
 
-    lax.fori_loop(0, chunks + LAG["h"], iteration, 0)
+    lax.fori_loop(0, chunks + lags["h"], iteration, 0)
 
     sent = (
         y1_send,
@@ -280,7 +285,8 @@
         await_bytes(ref, send_sem.at[stage])
 
 
-def step_call(win_slots, lose_slots, collective_id, table, rates, ones, twos, *blocks):
+def step_call(plan, table, rates, ones, twos, *blocks):
+    member_slots, order, lags = PLANS[plan]
     tokens, cotangent, weight, first, second = blocks
     rows, width = weight.shape
     cols = width // SPLIT
@@ -293,12 +299,12 @@
     y2 = pltpu.VMEM((chunks, 2, 2, ROWS, cols), kind)
     beside = pltpu.VMEM((chunks, ROWS, cols), kind)
     q1 = pltpu.VMEM((chunks, QUAD, 3, ROWS, part), kind)
-    z1 = pltpu.VMEM((chunks, LEVELS, win_slots, 3, ROWS // LEVELS, part), kind)
-    z2 = pltpu.VMEM((chunks, LEVELS, lose_slots, 3, ROWS // LEVELS, part), kind)
+    z1 = pltpu.VMEM((chunks, LEVELS, member_slots, 3, ROWS // LEVELS, part), kind)
+    z2 = pltpu.VMEM((chunks, LEVELS, member_slots, 3, ROWS // LEVELS, part), kind)
     q2 = pltpu.VMEM((chunks, QUAD, LEVELS, 3, ROWS // LEVELS, part), kind)
     dma = pltpu.SemaphoreType.DMA
     return pl.pallas_call(
-        functools.partial(step_kernel, win_slots, lose_slots),
+        functools.partial(step_kernel, member_slots, order, lags),
         out_shape=(
             jax.ShapeDtypeStruct(weight.shape, jnp.float32),
             jax.ShapeDtypeStruct(weight.shape, kind),
@@ -321,7 +327,7 @@
             z2,
             q2,
             q2,
-            pltpu.VMEM((LAG["d"] + 1, 4, ROWS, cols), jnp.float32),
+            pltpu.VMEM((lags["d"] + 1, 4, ROWS, cols), jnp.float32),
             pltpu.VMEM(q1.shape[1:], kind),
             pltpu.VMEM(z1.shape[1:], kind),
             pltpu.VMEM(z2.shape[1:], kind),
@@ -335,7 +341,7 @@
             dma((chunks,)),
         ],
         compiler_params=pltpu.CompilerParams(
-            collective_id=collective_id,
+            collective_id=plan,
             has_side_effects=True,
             vmem_limit_bytes=63 * 2**20,
         ),
@@ -371,7 +377,8 @@
     table = jnp.concatenate(
         [chosen.reshape(-1), wanted.reshape(-1), slot.reshape(-1), loser.astype(jnp.int32)]
     )
-    return table, loser, equal
+    most = jnp.max(jnp.maximum(jnp.sum(win, axis=1), jnp.sum(lose, axis=1)))
+    return table, most, loser, equal
 
 
 def on_device(
@@ -386,11 +393,11 @@
     sources,
     perturb,
 ):
-    table, loser, equal = routes(sources)
-    new_weight, new_first, new_second = step_call(
-        QUAD,
-        QUAD,
-        0,
+    table, most, loser, equal = routes(sources)
+    plan = jnp.clip(most - PLANS[0][0], 0, len(PLANS) - 1)
+    new_weight, new_first, new_second = lax.switch(
+        plan,
+        [functools.partial(step_call, which) for which in range(len(PLANS))],
         table,
         learn_rate,
         beta_one,

time: 207 us -> 147 us (0.71)
  Pallas kernels: 195 us -> 132 us
    pallas_call x1, Pallas kernels: 195 us -> 132 us  [step_call(): pl.pallas_call(functools.partial(step_kernel, member_slots, order, lags),...]
where the time goes in v2:
time: 147 us; the launch traced here: 146 us
  Pallas kernels  132 us (90%)
  local copies, waits for them, and re-layouts  7.18 us (5%)
  other arithmetic  5.46 us (4%)
    pallas_call x1, Pallas kernels, step_call(): pl.pallas_call(functools.partial(step_kernel, member_slots, order, lags),...  132 us
    unnamed x13, local copies, waits for them, and re-layouts  5.84 us

profile of v2, /device:TPU:1, one launch (start us, length us, event | category | flops | bytes accessed | tf_op | source)
XLA Modules:
  0.0 146.4 jit_solution(1716848773014173740)
XLA Ops:
  0.6 0.7 fusion.7
  1.3 0.1 reshape.95
  1.4 0.1 copy.17
  1.5 0.8 fusion.1
  2.2 0.1 reshape.94
  2.3 0.1 copy.14
  2.4 0.1 fusion.4
  2.5 0.1 multiply_reduce_fusion.1
  2.6 0.1 copy.19
  2.6 0.1 reshape.92
  2.7 0.8 select_reduce_fusion.1
  3.6 0.1 broadcast_in_dim.96
  3.7 0.1 copy.20
  3.7 0.1 copy.18
  3.8 0.1 copy.15
  4.0 0.1 copy.16
  4.1 0.1 reshape.91
  4.1 0.1 copy.21
  4.2 0.1 reshape.93
  4.3 0.1 copy.22
  4.4 0.1 reduce_sum.81
  4.5 0.7 compare_select_fusion
  5.1 0.1 pad_add_fusion
  5.2 0.1 reduce_sum.75
  5.3 0.1 reduce_sum.74
  5.5 0.6 maximum_reduce_fusion
  6.8 0.0 copy-start.3
  6.8 0.0 copy-start.2
  6.8 0.0 copy-start.4
  6.8 132.4 %conditional.1 = (f32[1,512,1024]{2,1,0:T(8,128)}, bf16[1,512,1024]{2,1,0:T(8,128)(2,1)}, bf16[1,512,1024]{2,1,0:T(8,128)(2,1)}) conditional(s32[]{:T(128)} %clamp.3, (bf16[1,512,4096]{2,1,0:T(8,128)(2,1)}, bf16[1,512,1024]{2,1,0:T(8,128)(2,1)}, f32[1,512,1024]{2,1,0:T(8,128)}, bf16[1,512,1024]{2,1,0:T(8,128)(2,1)}, ...), branch_computations={%region_9.10_spmd, %region_10.11_spmd, %region_11.12_spmd} | conditional | bytes 24 | solution.py:398
  6.8 132.4 %branch_0_fun.1 = (f32[512,1024]{1,0:T(8,128)}, bf16[512,1024]{1,0:T(8,128)(2,1)}, bf16[512,1024]{1,0:T(8,128)(2,1)}) custom-call(s32[128]{0:T(128)S(1)} %get-tuple-element.81.table, f32[32]{0:T(128)} %get-tuple-element.82.rates, f32[32]{0:T(128)} %get-tuple-element.83.decays_one, f32[32]{0:T(128)} %get-tuple-element.84.decays_two, ...), custom_call_target="tpu_custom_call" | custom-call | tf_op jit(solution)/shard_map/cond/branch_0_fun/pallas_call | solution.py:306
  139.2 0.0 copy-done.3
  139.2 0.8 select_reduce_fusion
  140.1 0.0 copy-done.2
  140.1 0.0 copy-done.4
  140.1 0.5 log_select_fusion
  140.6 0.0 copy-start
  140.6 3.2 %copy.35 = f32[1,512,1024]{2,1,0:T(8,128)} copy(f32[1,512,1024]{2,1,0:T(8,128)} %get-tuple-element.146) | data formatting | bytes 4194304
  143.9 0.0 copy-done
  143.9 0.0 copy-start.1
  143.9 1.0 copy.36
  144.8 0.6 copy-done.1
  145.5 1.0 copy.37
  (6 shorter events, 0.1 us)
Async XLA Ops:
  6.8 132.5 %copy-start.3 = (s32[32]{0:T(128)S(1)}, s32[32]{0:T(128)}, u32[]{:S(2)}) copy-start(s32[32]{0:T(128)} %param.21) | copy-start | bytes 388
  6.8 133.3 %copy-start.2 = (f32[32]{0:T(128)S(1)}, f32[32]{0:T(128)}, u32[]{:S(2)}) copy-start(f32[32]{0:T(128)} %param.18) | copy-start | bytes 388
  6.8 133.3 %copy-start.4 = (s32[32]{0:T(128)S(1)}, s32[32]{0:T(128)}, u32[]{:S(2)}) copy-start(s32[32]{0:T(128)} %param.22) | copy-start | bytes 388
  140.6 3.3 %copy-start = (bf16[1,512,1024]{2,1,0:T(8,128)(2,1)S(1)}, bf16[1,512,1024]{2,1,0:T(8,128)(2,1)}, u32[]{:S(2)}) copy-start(bf16[1,512,1024]{2,1,0:T(8,128)(2,1)} %get-tuple-element.147) | copy-start | bytes 3145732
  143.9 1.6 %copy-start.1 = (bf16[1,512,1024]{2,1,0:T(8,128)(2,1)S(1)}, bf16[1,512,1024]{2,1,0:T(8,128)(2,1)}, u32[]{:S(2)}) copy-start(bf16[1,512,1024]{2,1,0:T(8,128)(2,1)} %get-tuple-element.148) | copy-start | bytes 3145732

commit v3 on v2

v3 whole, which is shorter than its diff:
```python
import functools
import math

import jax
import jax.numpy as jnp
from jax import lax
from jax.experimental import pallas as pl
from jax.experimental.pallas import tpu as pltpu
from jax.sharding import PartitionSpec as P

MESH = pl.DeviceIdType.MESH
ROWS = 128
SPLIT = 2
LEVELS = 8
QUAD = 4
RING = 4
EARLY = 4
PLANS = (
    (2, 2, "fchrdgbeap", dict(a=0, b=1, c=2, d=3, e=4, f=6, g=7, h=9, p=0, r=2)),
    (2, 3, "redchpbfga", dict(a=0, b=1, c=2, d=3, e=4, f=5, g=7, h=9, p=0, r=2)),
    (3, 3, "gphredcbaf", dict(a=0, b=1, c=2, d=3, e=4, f=5, g=8, h=10, p=0, r=1)),
    (4, 4, "rbpedfaghc", dict(a=0, b=1, c=2, d=3, e=4, f=7, g=9, h=9, p=0, r=1)),
)


def twentieth_power(value):
    square = value * value
    fourth = square * square
    eighth = fourth * fourth
    return eighth * eighth * fourth


def adam(master, first, second, gradient, rate, decay_one, decay_two):
    scale_one = 1.0 / (1.0 - twentieth_power(decay_one))
    scale_two = 1.0 / (1.0 - twentieth_power(decay_two))
    moment_one = decay_one * first + (1.0 - decay_one) * gradient
    moment_two = decay_two * second + (1.0 - decay_two) * gradient * gradient
    updated = master - rate * (
        (moment_one * scale_one) / (jnp.sqrt(moment_two * scale_two) + 1e-08) + 0.1 * master
    )
    return updated, moment_one, moment_two


def step_kernel(
    win_slots,
    lose_slots,
    order,
    lags,
    table,
    rates,
    decays_one,
    decays_two,
    tokens_in,
    cotangent_in,
    weight_in,
    first_in,
    second_in,
    weight_out,
    first_out,
    second_out,
    tokens,
    cotangent,
    weight,
    first,
    second,
    out_weight,
    out_first,
    out_second,
    y1_send,
    y1_recv,
    y2_send,
    y2_recv,
    x_send,
    x_recv,
    q1_send,
    q1_recv,
    z1_send,
    z1_recv,
    z2_send,
    z2_recv,
    q2_send,
    q2_recv,
    g1_send,
    g1_recv,
    g2_send,
    g2_recv,
    terms,
    q1_held,
    z1_held,
    z2_held,
    g1_held,
    load_sem,
    out_sem,
    send_sem,
    y1_sem,
    y2_sem,
    x_sem,
    q1_sem,
    z1_sem,
    z2_sem,
    q2_sem,
    g1_sem,
    g2_sem,
):
    chunks = y1_send.shape[0]
    cols = y1_send.shape[3]
    plain = chunks - EARLY
    part = cols // QUAD
    own_rows = weight.shape[0]
    slots = terms.shape[0]
    member = lax.axis_index("member")
    shard = lax.axis_index("shard")
    level, mine = member // QUAD, lax.rem(member, QUAD)
    y, x_lo = shard // 2, lax.rem(shard, 2)
    y_next, y_prev = lax.rem(y + 1, RING), lax.rem(y + RING - 1, RING)
    y_far = lax.rem(y + 2, RING)

    def on_shard(at_y, at_x):
        return {"member": member, "shard": at_y * 2 + at_x}

    def on_member(at_level, at_quad):
        return {"member": at_level * QUAD + at_quad, "shard": shard}

    up, down = on_shard(y_next, x_lo), on_shard(y_prev, x_lo)
    beside = on_shard(y, 1 - x_lo)
    quads = [lax.rem(mine + d, QUAD) for d in range(1, QUAD)]
    levels = [lax.rem(level + d, LEVELS) for d in (4, 3, 5, 2, 6, 1, 7)]

    row_parts = own_rows // ROWS
    blocks = tokens.shape[1] // own_rows

    def load(src, dst, which):
        pltpu.make_async_copy(src, dst, load_sem.at[which]).start()

    def load_tokens(part_of_rows):
        for b in range(blocks):
            here = pl.ds(b * own_rows + part_of_rows * ROWS, ROWS)
            load(tokens_in.at[:, here], tokens.at[:, here], part_of_rows)

    load(cotangent_in, cotangent, row_parts)
    load_tokens(0)
    load(weight_in, weight, row_parts + 1)
    load(first_in, first, row_parts + 2)
    load(second_in, second, row_parts + 3)
    for r in range(1, row_parts):
        load_tokens(r)

    peers = [up, down, beside]
    peers += [on_member(level, q) for q in quads]
    peers += [on_member(z, mine) for z in levels]
    barrier = pltpu.get_barrier_semaphore()
    for peer in peers:
        pl.semaphore_signal(barrier, inc=1, device_id=peer, device_id_type=MESH)
    pl.semaphore_wait(barrier, len(peers))

    def send(src, dst, stage, recv, device):
        pltpu.make_async_remote_copy(
            src_ref=src,
            dst_ref=dst,
            send_sem=send_sem.at[stage],
            recv_sem=recv,
            device_id=device,
            device_id_type=MESH,
        ).start()

    def await_bytes(ref, sem):
        pltpu.make_async_copy(ref, ref, sem).wait()

    def place(k):
        row = pl.multiple_of((k // SPLIT) * ROWS, ROWS)
        col = pl.multiple_of(lax.rem(k, SPLIT) * cols, cols)
        return row, col

    def term(k, at_y, at_x):
        row, col = place(k)
        start = pl.multiple_of((at_y * 2 + at_x) * own_rows + row, ROWS)
        return lax.dot_general(
            tokens[:, pl.ds(start, ROWS)],
            cotangent[:, pl.ds(col, cols)],
            (((0,), (0,)), ((), ())),
            preferred_element_type=jnp.float32,
        )

    def stage_a(k):
        slot = lax.rem(k, slots)

        @pl.when(k == 0)
        def _():
            await_bytes(cotangent, load_sem.at[row_parts])

        @pl.when(lax.rem(k, SPLIT) == 0)
        def _():
            await_bytes(tokens.at[:, pl.ds(0, blocks * ROWS)], load_sem.at[k // SPLIT])

        y1_send[k, 0] = term(k, y_far, 0).astype(jnp.bfloat16)
        send(y1_send.at[k, 0], y1_recv.at[k, 0], 0, y1_sem.at[k, 0], up)
        y1_send[k, 1] = term(k, y_far, 1).astype(jnp.bfloat16)
        send(y1_send.at[k, 1], y1_recv.at[k, 1], 0, y1_sem.at[k, 1], down)
        y2_send[k, 0, 1] = term(k, y_next, 1).astype(jnp.bfloat16)
        send(y2_send.at[k, 0, 1], y2_recv.at[k, 0, 1], 1, y2_sem.at[k, 0], up)
        y2_send[k, 1, 0] = term(k, y_prev, 0).astype(jnp.bfloat16)
        send(y2_send.at[k, 1, 0], y2_recv.at[k, 1, 0], 1, y2_sem.at[k, 1], down)
        terms[slot, 0] = term(k, y_next, 0)
        terms[slot, 1] = term(k, y_prev, 1)
        terms[slot, 2] = term(k, y, 1 - x_lo)
        terms[slot, 3] = term(k, y, x_lo)

    def stage_b(k):
        slot = lax.rem(k, slots)
        await_bytes(y1_recv.at[k, 0], y1_sem.at[k, 0])
        y2_send[k, 0, 0] = (terms[slot, 0] + y1_recv[k, 0].astype(jnp.float32)).astype(jnp.bfloat16)
        send(y2_send.at[k, 0, 0], y2_recv.at[k, 0, 0], 1, y2_sem.at[k, 0], up)
        await_bytes(y1_recv.at[k, 1], y1_sem.at[k, 1])
        y2_send[k, 1, 1] = (terms[slot, 1] + y1_recv[k, 1].astype(jnp.float32)).astype(jnp.bfloat16)
        send(y2_send.at[k, 1, 1], y2_recv.at[k, 1, 1], 1, y2_sem.at[k, 1], down)

    def stage_c(k):
        slot = lax.rem(k, slots)
        await_bytes(y2_recv.at[k, 0], y2_sem.at[k, 0])
        await_bytes(y2_recv.at[k, 1], y2_sem.at[k, 1])

        def total(which, at_x):
            return (
                terms[slot, which]
                + y2_recv[k, 0, at_x].astype(jnp.float32)
                + y2_recv[k, 1, at_x].astype(jnp.float32)
            )

        x_send[k] = total(2, 1 - x_lo).astype(jnp.bfloat16)
        send(x_send.at[k], x_recv.at[k], 2, x_sem.at[k], beside)
        terms[slot, 3] = total(3, x_lo)

    def pack(k, arrays):
        for q in range(QUAD):
            for a in range(3):
                q1_send[k, q, a] = arrays[a][:, q * part : (q + 1) * part]
        for q in quads:
            send(q1_send.at[k, q], q1_recv.at[k, mine], 3, q1_sem.at[k], on_member(level, q))
        q1_recv[k, mine] = q1_send[k, mine]

    def spread(k):
        await_bytes(q1_recv.at[k, pl.ds(0, QUAD - 1)], q1_sem.at[k])
        q1_held[...] = q1_recv[k]
        for j in range(win_slots):
            chosen = q1_held[table[level * QUAD + j]]
            for z in range(LEVELS):
                z1_send[k, z, j] = chosen[:, z * 16 : (z + 1) * 16, :]
        for z in levels:
            send(z1_send.at[k, z], z1_recv.at[k, level], 4, z1_sem.at[k], on_member(z, mine))
        z1_recv[k, level] = z1_send[k, level]

    def stage_p(k):
        @pl.when(k == plain)
        def _():
            await_bytes(weight, load_sem.at[row_parts + 1])
            await_bytes(first, load_sem.at[row_parts + 2])
            await_bytes(second, load_sem.at[row_parts + 3])

        row, col = place(k)
        here = (pl.ds(row, ROWS), pl.ds(col, cols))
        pack(k, (weight[here].astype(jnp.bfloat16), first[here], second[here]))

    def stage_d(k):
        slot = lax.rem(k, slots)
        row, col = place(k)
        here = (pl.ds(row, ROWS), pl.ds(col, cols))
        await_bytes(x_recv.at[k], x_sem.at[k])
        gradient = terms[slot, 3] + x_recv[k].astype(jnp.float32)
        updated, moment_one, moment_two = adam(
            weight[here],
            first[here].astype(jnp.float32),
            second[here].astype(jnp.float32),
            gradient,
            jnp.full((1, cols), rates[member], jnp.float32),
            jnp.full((1, cols), decays_one[member], jnp.float32),
            jnp.full((1, cols), decays_two[member], jnp.float32),
        )
        out_weight[here] = updated
        out_first[here] = moment_one.astype(jnp.bfloat16)
        out_second[here] = moment_two.astype(jnp.bfloat16)

        @pl.when(k < plain)
        def _():
            pack(k, (out_weight[here].astype(jnp.bfloat16), out_first[here], out_second[here]))

        @pl.when(k >= plain)
        def _():
            e = k - plain
            for q in range(QUAD):
                g1_send[e, q] = gradient[:, q * part : (q + 1) * part].astype(jnp.bfloat16)
            for q in quads:
                send(g1_send.at[e, q], g1_recv.at[e, mine], 7, g1_sem.at[e], on_member(level, q))
            g1_recv[e, mine] = g1_send[e, mine]

    def stage_e(k):
        @pl.when(k < plain)
        def _():
            spread(k)

        @pl.when(k >= plain)
        def _():
            e = k - plain
            await_bytes(g1_recv.at[e, pl.ds(0, QUAD - 1)], g1_sem.at[e])
            g1_held[...] = g1_recv[e]
            for j in range(win_slots):
                chosen = g1_held[table[level * QUAD + j]]
                for z in range(LEVELS):
                    g2_send[e, z, j] = chosen[z * 16 : (z + 1) * 16, :]
            for z in levels:
                send(g2_send.at[e, z], g2_recv.at[e, level], 8, g2_sem.at[e], on_member(z, mine))
            g2_recv[e, level] = g2_send[e, level]

    def stage_f(k):
        await_bytes(z1_recv.at[k, pl.ds(0, LEVELS - 1)], z1_sem.at[k])
        z1_held[...] = z1_recv[k]

        @pl.when(k >= plain)
        def _():
            e = k - plain
            await_bytes(g2_recv.at[e, pl.ds(0, LEVELS - 1)], g2_sem.at[e])

            def step_level(z, carry):
                for j in range(win_slots):
                    who = z * QUAD + table[z * QUAD + j]
                    stepped = adam(
                        z1_held[z, j, 0].astype(jnp.float32),
                        z1_held[z, j, 1].astype(jnp.float32),
                        z1_held[z, j, 2].astype(jnp.float32),
                        g2_recv[e, z, j].astype(jnp.float32),
                        jnp.full((1, part), rates[who], jnp.float32),
                        jnp.full((1, part), decays_one[who], jnp.float32),
                        jnp.full((1, part), decays_two[who], jnp.float32),
                    )
                    for a in range(3):
                        z1_held[z, j, a] = stepped[a].astype(jnp.bfloat16)
                return carry

            lax.fori_loop(0, LEVELS, step_level, 0)

        for z in range(LEVELS):
            for j in range(lose_slots):
                source = table[32 + z * QUAD + j]
                z2_send[k, z, j] = z1_held[source // QUAD, lax.rem(source, QUAD)]
        for z in levels:
            send(z2_send.at[k, z], z2_recv.at[k, level], 5, z2_sem.at[k], on_member(z, mine))
        z2_recv[k, level] = z2_send[k, level]

    def stage_g(k):
        await_bytes(z2_recv.at[k, pl.ds(0, LEVELS - 1)], z2_sem.at[k])
        z2_held[...] = z2_recv[k]
        for q in range(QUAD):
            slot = table[64 + level * QUAD + q]
            for z in range(LEVELS):
                q2_send[k, q, z] = z2_held[z, slot]
        for q in quads:
            send(q2_send.at[k, q], q2_recv.at[k, mine], 6, q2_sem.at[k], on_member(level, q))
        q2_recv[k, mine] = q2_send[k, mine]

    outs = ((out_weight, weight_out), (out_first, first_out), (out_second, second_out))

    def stage_h(k):
        row, col = place(k)
        await_bytes(q2_recv.at[k, pl.ds(0, QUAD - 1)], q2_sem.at[k])
        taken = jnp.full((1, part), table[96 + member], jnp.int32) != 0
        for q in range(QUAD):
            for a in range(3):
                ref = outs[a][0]
                here = (pl.ds(row, ROWS), pl.ds(col + q * part, part))
                copied = q2_recv[k, q, :, a].reshape(ROWS, part).astype(jnp.float32)
                kept = ref[here].astype(jnp.float32)
                ref[here] = jnp.where(taken, copied, kept).astype(ref.dtype)
        for a in range(3):
            here = (pl.ds(row, ROWS), pl.ds(col, cols))
            pltpu.make_async_copy(outs[a][0].at[here], outs[a][1].at[here], out_sem.at[a]).start()

    stages = dict(
        a=stage_a,
        b=stage_b,
        c=stage_c,
        d=stage_d,
        e=stage_e,
        f=stage_f,
        g=stage_g,
        h=stage_h,
        p=stage_p,
        r=spread,
    )

    def iteration(i, carry):
        for name in order:
            lowest = plain if name in "pr" else 0
            k = i - lags[name] + lowest

            @pl.when((k >= lowest) & (k < chunks))
            def _():
                stages[name](k)

        return carry

    lax.fori_loop(0, chunks + lags["h"], iteration, 0)

    sent = (
        y1_send,
        y2_send,
        x_send,
        q1_send.at[:, pl.ds(0, QUAD - 1)],
        z1_send.at[:, pl.ds(0, LEVELS - 1)],
        z2_send.at[:, pl.ds(0, LEVELS - 1)],
        q2_send.at[:, pl.ds(0, QUAD - 1)],
        g1_send.at[:, pl.ds(0, QUAD - 1)],
        g2_send.at[:, pl.ds(0, LEVELS - 1)],
    )
    for stage, ref in enumerate(sent):
        await_bytes(ref, send_sem.at[stage])
    for a in range(3):
        await_bytes(outs[a][0], out_sem.at[a])


def step_call(plan, table, rates, ones, twos, *blocks):
    win_slots, lose_slots, order, lags = PLANS[plan]
    tokens, cotangent, weight, first, second = blocks
    rows, width = weight.shape
    cols = width // SPLIT
    chunks = rows // ROWS * SPLIT
    part = cols // QUAD
    kind = jnp.bfloat16
    scalars = pl.BlockSpec(memory_space=pltpu.SMEM)
    anywhere = pl.BlockSpec(memory_space=pl.ANY)
    like = [pltpu.VMEM(block.shape, block.dtype) for block in blocks]
    y1 = pltpu.VMEM((chunks, 2, ROWS, cols), kind)
    y2 = pltpu.VMEM((chunks, 2, 2, ROWS, cols), kind)
    beside = pltpu.VMEM((chunks, ROWS, cols), kind)
    q1 = pltpu.VMEM((chunks, QUAD, 3, ROWS, part), kind)
    z1 = pltpu.VMEM((chunks, LEVELS, win_slots, 3, ROWS // LEVELS, part), kind)
    z2 = pltpu.VMEM((chunks, LEVELS, lose_slots, 3, ROWS // LEVELS, part), kind)
    q2 = pltpu.VMEM((chunks, QUAD, LEVELS, 3, ROWS // LEVELS, part), kind)
    g1 = pltpu.VMEM((EARLY, QUAD, ROWS, part), kind)
    g2 = pltpu.VMEM((EARLY, LEVELS, win_slots, ROWS // LEVELS, part), kind)
    dma = pltpu.SemaphoreType.DMA
    return pl.pallas_call(
        functools.partial(step_kernel, win_slots, lose_slots, order, lags),
        out_shape=(
            jax.ShapeDtypeStruct(weight.shape, jnp.float32),
            jax.ShapeDtypeStruct(weight.shape, kind),
            jax.ShapeDtypeStruct(weight.shape, kind),
        ),
        in_specs=[scalars] * 4 + [anywhere] * 5,
        out_specs=(anywhere,) * 3,
        scratch_shapes=like
        + [like[2], like[3], like[4]]
        + [y1, y1, y2, y2, beside, beside, q1, q1, z1, z1, z2, z2, q2, q2, g1, g1, g2, g2]
        + [
            pltpu.VMEM((lags["d"] + 1, 4, ROWS, cols), jnp.float32),
            pltpu.VMEM(q1.shape[1:], kind),
            pltpu.VMEM(z1.shape[1:], kind),
            pltpu.VMEM(z2.shape[1:], kind),
            pltpu.VMEM(g1.shape[1:], kind),
            dma((rows // ROWS + 4,)),
            dma((3,)),
            dma((9,)),
            dma((chunks, 2)),
            dma((chunks, 2)),
            dma((chunks,)),
            dma((chunks,)),
            dma((chunks,)),
            dma((chunks,)),
            dma((chunks,)),
            dma((EARLY,)),
            dma((EARLY,)),
        ],
        compiler_params=pltpu.CompilerParams(
            collective_id=plan,
            has_side_effects=True,
            vmem_limit_bytes=63 * 2**20,
        ),
    )(table, rates, ones, twos, *blocks)


def route_kernel(sources, rates, perturb, table, plan, log_rate, winner, place):
    members = sources.shape[0]

    def clear(m, carry):
        winner[m] = 0
        for part in range(4):
            table[part * members + m] = 0
        return carry

    lax.fori_loop(0, members, clear, 0)

    def mark(m, carry):
        @pl.when(sources[m] != m)
        def _():
            winner[sources[m]] = 1

        return carry

    lax.fori_loop(0, members, mark, 0)

    def rank(z, most):
        wins = losses = jnp.int32(0)
        for q in range(QUAD):
            m = z * QUAD + q
            won = winner[m]
            lost = (sources[m] != m).astype(jnp.int32)
            place[m] = z * QUAD + wins
            table[2 * members + m] = jnp.where(lost != 0, losses, 0)
            table[3 * members + m] = lost

            @pl.when(won != 0)
            def _():
                table[z * QUAD + wins] = q

            wins += won
            losses += lost
        return jnp.maximum(most[0], wins), jnp.maximum(most[1], losses)

    wins, losses = lax.fori_loop(0, members // QUAD, rank, (jnp.int32(0), jnp.int32(0)))
    plan[0] = jnp.where(
        wins > 3, 3, jnp.where(losses > 3, 3, jnp.where(wins > 2, 2, jnp.where(losses > 2, 1, 0)))
    )

    def want(m, carry):
        @pl.when(sources[m] != m)
        def _():
            slot = (m // QUAD) * QUAD + table[2 * members + m]
            table[members + slot] = place[sources[m]]

        return carry

    lax.fori_loop(0, members, want, 0)
    lane = lax.broadcasted_iota(jnp.int32, log_rate.shape, 1)

    def gather(m, carry):
        rate, shift = carry
        source = sources[m]
        moved = jnp.where(source != m, perturb[m] - 1, 0)
        here = lane == m
        return jnp.where(here, rates[source], rate), jnp.where(here, moved, shift)

    start = (jnp.ones(log_rate.shape, jnp.float32), jnp.zeros(log_rate.shape, jnp.int32))
    rate, shift = lax.fori_loop(0, members, gather, start)
    log_rate[...] = jnp.log(rate) + shift.astype(jnp.float32) * math.log(2.0)


def route_call(sources, rates, perturb):
    members = sources.shape[0]
    scalars = pl.BlockSpec(memory_space=pltpu.SMEM)
    return pl.pallas_call(
        route_kernel,
        out_shape=(
            jax.ShapeDtypeStruct((4 * members,), jnp.int32),
            jax.ShapeDtypeStruct((1,), jnp.int32),
            jax.ShapeDtypeStruct((1, members), jnp.float32),
        ),
        in_specs=[scalars] * 3,
        out_specs=(scalars, scalars, pl.BlockSpec(memory_space=pltpu.VMEM)),
        scratch_shapes=[pltpu.SMEM((members,), jnp.int32)] * 2,
    )(sources, rates, perturb)


def copy_kernel(arrays, *refs):
    sources, targets, held = (refs[i * arrays : (i + 1) * arrays] for i in range(3))
    read_sem, write_sem = refs[3 * arrays :]
    pieces = read_sem.shape[1]
    reads, writes = [], []
    for p in range(pieces):
        for a in range(arrays):
            rows = sources[a].shape[0] // pieces
            here = pl.ds(p * rows, rows)
            reads.append(
                pltpu.make_async_copy(sources[a].at[here], held[a].at[here], read_sem.at[a, p])
            )
            writes.append(
                pltpu.make_async_copy(held[a].at[here], targets[a].at[here], write_sem.at[a, p])
            )
    for read in reads:
        read.start()
    for read, write in zip(reads, writes):
        read.wait()
        write.start()
    for write in writes:
        write.wait()


def copy_call(*arrays):
    anywhere = pl.BlockSpec(memory_space=pl.ANY)
    pieces = pltpu.SemaphoreType.DMA((len(arrays), 4))
    return pl.pallas_call(
        functools.partial(copy_kernel, len(arrays)),
        out_shape=tuple(jax.ShapeDtypeStruct(a.shape, a.dtype) for a in arrays),
        in_specs=[anywhere] * len(arrays),
        out_specs=(anywhere,) * len(arrays),
        scratch_shapes=[pltpu.VMEM(a.shape, a.dtype) for a in arrays] + [pieces, pieces],
        compiler_params=pltpu.CompilerParams(vmem_limit_bytes=32 * 2**20),
    )(*arrays)


def on_device(
    tokens,
    cotangent,
    weight,
    first_moment,
    second_moment,
    learn_rate,
    beta_one,
    beta_two,
    sources,
    perturb,
):
    table, plan, log_rate = route_call(sources, learn_rate, perturb)
    stepped = lax.switch(
        plan[0],
        [functools.partial(step_call, which) for which in range(len(PLANS))],
        table,
        learn_rate,
        beta_one,
        beta_two,
        tokens[0],
        cotangent[0],
        weight[0],
        first_moment[0],
        second_moment[0],
    )
    new_weight, new_first, new_second = copy_call(*stepped)
    return new_weight[None], new_first[None], new_second[None], log_rate[0]


def solution(mesh):
    block = P("member", "shard", None)
    return jax.shard_map(
        on_device,
        mesh=mesh,
        in_specs=(block,) * 5 + (P(),) * 5,
        out_specs=(block, block, block, P()),
        check_vma=False,
    )
```

time: 147 us -> 147 us (level)
  Pallas kernels: 132 us -> 145 us
  local copies, waits for them, and re-layouts: 7.18 us -> 0 us
  other arithmetic: 5.46 us -> 0 us
    pallas_call x1 -> x3, Pallas kernels: 132 us -> 145 us  [the longest x1 138 us: step_call(): pl.pallas_call(functools.partial(step_kernel, win_slots, lose_slots, orde...]
    unnamed x13 -> x0, local copies, waits for them, and re-layouts: 5.84 us -> none
    reduce_sum x6 -> x0, other arithmetic: 2.03 us -> none  [the longest x1 0.84 us: routes(): source_place = jnp.sum(jnp.where(equal, place[None, :], 0), axis=1)]
where the time goes in v3:
time: 147 us; the launch traced here: 146 us
  Pallas kernels  145 us (99%)
  between operations  1.48 us (1%)
    pallas_call x1, Pallas kernels, step_call(): pl.pallas_call(functools.partial(step_kernel, win_slots, lose_slots, orde...  138 us
    pallas_call x1, Pallas kernels, copy_call(): pl.pallas_call(functools.partial(copy_kernel, len(arrays)), out_shape=tup...  3.54 us

profile of v3, /device:TPU:1, one launch (start us, length us, event | category | flops | bytes accessed | tf_op | source)
XLA Modules:
  0.0 146.5 jit_solution(5607382415594468841)
XLA Ops:
  0.6 2.9 %shard_map.129 = (s32[128]{0:T(128)S(1)}, s32[1]{0:T(128)}, f32[1,32]{1,0:T(1,128)}) custom-call(s32[32]{0:T(128)} %sources.1, f32[32]{0:T(128)} %rates.1, s32[32]{0:T(128)} %perturb.1), custom_call_target="tpu_custom_call" | custom-call | tf_op jit(solution)/shard_map/pallas_call | solution.py:548
  4.2 138.6 %conditional.1 = ((f32[512,1024]{1,0:T(8,128)}, bf16[512,1024]{1,0:T(8,128)(2,1)}, bf16[512,1024]{1,0:T(8,128)(2,1)})) conditional(s32[]{:T(128)} %bitcast, (s32[128]{0:T(128)S(1)}, f32[32]{0:T(128)}, f32[32]{0:T(128)}, f32[32]{0:T(128)}, bf16[512,4096]{1,0:T(8,128)(2,1)}, /*index=5*/bf16[512,1024]{1,0:T(8,128)(2,1)}, ...), branch_computations={%region_0.0_spmd, %region_1.0_spmd, %region_2.0_spmd, %region_3.0_... | conditional | bytes 8 | solution.py:611
  4.2 138.1 %branch_2_fun.1 = (f32[512,1024]{1,0:T(8,128)}, bf16[512,1024]{1,0:T(8,128)(2,1)}, bf16[512,1024]{1,0:T(8,128)(2,1)}) custom-call(s32[128]{0:T(128)S(1)} %get-tuple-element.90.table, f32[32]{0:T(128)} %get-tuple-element.91.rates, f32[32]{0:T(128)} %get-tuple-element.92.decays_one, f32[32]{0:T(128)} %get-tuple-element.93.decays_two, ...), custom_call_target="tpu_custom_call" | custom-call | tf_op jit(solution)/shard_map/cond/branch_2_fun/pallas_call | solution.py:440
  142.8 3.5 %shard_map.130 = (f32[512,1024]{1,0:T(8,128)}, bf16[512,1024]{1,0:T(8,128)(2,1)}, bf16[512,1024]{1,0:T(8,128)(2,1)}) custom-call(f32[512,1024]{1,0:T(8,128)} %get-tuple-element.123.refs_0_, bf16[512,1024]{1,0:T(8,128)(2,1)} %get-tuple-element.124.refs_1_, bf16[512,1024]{1,0:T(8,128)(2,1)} %get-tuple-element.125.refs_2_), custom_call_target="tpu_custom_call" | custom-call | tf_op jit(solution)/shard_map/pallas_call | solution.py:588

commit v4 on v3

--- a/solution.py
+++ b/solution.py
@@ -14,12 +14,12 @@
 LEVELS = 8
 QUAD = 4
 RING = 4
-EARLY = 4
 PLANS = (
-    (2, 2, "fchrdgbeap", dict(a=0, b=1, c=2, d=3, e=4, f=6, g=7, h=9, p=0, r=2)),
-    (2, 3, "redchpbfga", dict(a=0, b=1, c=2, d=3, e=4, f=5, g=7, h=9, p=0, r=2)),
-    (3, 3, "gphredcbaf", dict(a=0, b=1, c=2, d=3, e=4, f=5, g=8, h=10, p=0, r=1)),
-    (4, 4, "rbpedfaghc", dict(a=0, b=1, c=2, d=3, e=4, f=7, g=9, h=9, p=0, r=1)),
+    (2, 2, True, 3, "sgfjtchdpibrea", dict(a=0, b=1, c=2, d=3, i=3, e=4, f=6, g=8, h=10, p=0, j=1, r=1, s=3, t=4)),
+    (2, 2, False, 3, "ftsrcpdbaegh", dict(a=0, b=1, c=2, d=3, e=4, f=6, g=8, h=11, p=0, r=2, s=3, t=4)),
+    (2, 3, False, 3, "efpdrctghsba", dict(a=0, b=1, c=2, d=3, e=4, f=6, g=8, h=11, p=0, r=1, s=2, t=5)),
+    (3, 3, False, 2, "esdctprbhgaf", dict(a=0, b=1, c=2, d=3, e=4, f=5, g=7, h=10, p=0, r=1, s=3, t=5)),
+    (4, 4, False, 1, "fdphtscbearg", dict(a=0, b=1, c=2, d=3, e=3, f=5, g=7, h=9, p=0, r=0, s=3, t=7)),
 )
 
 
@@ -42,10 +42,7 @@
 
 
 def step_kernel(
-    win_slots,
-    lose_slots,
-    order,
-    lags,
+    plan,
     table,
     rates,
     decays_one,
@@ -84,11 +81,21 @@
     g1_recv,
     g2_send,
     g2_recv,
+    g3_send,
+    g3_recv,
+    g4_send,
+    g4_recv,
+    c1_recv,
+    c2_recv,
+    x1_send,
+    x2_send,
     terms,
     q1_held,
     z1_held,
     z2_held,
     g1_held,
+    g2_held,
+    g3_held,
     load_sem,
     out_sem,
     send_sem,
@@ -101,10 +108,15 @@
     q2_sem,
     g1_sem,
     g2_sem,
+    g3_sem,
+    g4_sem,
+    c1_sem,
+    c2_sem,
 ):
+    win_slots, lose_slots, by_chip, early, order, lags = plan
     chunks = y1_send.shape[0]
     cols = y1_send.shape[3]
-    plain = chunks - EARLY
+    plain = chunks - early
     part = cols // QUAD
     own_rows = weight.shape[0]
     slots = terms.shape[0]
@@ -123,6 +135,7 @@
 
     up, down = on_shard(y_next, x_lo), on_shard(y_prev, x_lo)
     beside = on_shard(y, 1 - x_lo)
+    column, core = mine // 2, lax.rem(mine, 2)
     quads = [lax.rem(mine + d, QUAD) for d in range(1, QUAD)]
     levels = [lax.rem(level + d, LEVELS) for d in (4, 3, 5, 2, 6, 1, 7)]
 
@@ -230,24 +243,121 @@
         send(x_send.at[k], x_recv.at[k], 2, x_sem.at[k], beside)
         terms[slot, 3] = total(3, x_lo)
 
+    def split(block, blocks, sem, chip_blocks, chip_sem, stage):
+        if by_chip:
+            for x in range(2):
+                q = x * 2 + 1 - core
+                there = on_member(level, column * 2 + 1 - core)
+                send(block.at[q], chip_blocks.at[x], stage, chip_sem, there)
+        else:
+            for q in quads:
+                send(block.at[q], blocks.at[mine], stage, sem, on_member(level, q))
+            blocks[mine] = block[mine]
+
+    def cross(block, chip_blocks, chip_sem, crossing, blocks, sem, held, stage):
+        await_bytes(chip_blocks, chip_sem)
+        for x in range(2):
+            held[x] = block[x * 2 + core]
+            held[2 + x] = chip_blocks[x]
+        other = (table[level * QUAD + column] + core) % 2
+        for x in range(2):
+            crossing[x] = held[other * 2 + x]
+        blocks[column] = crossing[column]
+        there = on_member(level, (1 - column) * 2 + core)
+        send(crossing.at[1 - column], blocks.at[column], stage, sem, there)
+
+    def select(blocks, sem, held, out, stage, targets, target_sem):
+        if by_chip:
+            await_bytes(blocks.at[pl.ds(0, 1)], sem)
+        else:
+            await_bytes(blocks.at[pl.ds(0, QUAD - 1)], sem)
+            held[...] = blocks[...]
+        for j in range(win_slots):
+            chosen = blocks[j] if by_chip else held[table[level * QUAD + j]]
+            for z in range(LEVELS):
+                out[z, j] = chosen[..., z * 16 : (z + 1) * 16, :]
+        for z in levels:
+            send(out.at[z], targets.at[level], stage, target_sem, on_member(z, mine))
+        targets[level] = out[level]
+
+    def forward(blocks, sem, held, out, stage, targets, target_sem):
+        await_bytes(blocks.at[pl.ds(0, LEVELS - 1)], sem)
+        held[...] = blocks[...]
+        for z in range(LEVELS):
+            for j in range(lose_slots):
+                source = table[32 + z * QUAD + j]
+                out[z, j] = held[source // QUAD, lax.rem(source, QUAD)]
+        for z in levels:
+            send(out.at[z], targets.at[level], stage, target_sem, on_member(z, mine))
+        targets[level] = out[level]
+
+    def deliver(blocks, sem, held, out, stage, targets, target_sem):
+        await_bytes(blocks.at[pl.ds(0, LEVELS - 1)], sem)
+        held[...] = blocks[...]
+        for q in range(QUAD):
+            slot = table[64 + level * QUAD + q]
+            for z in range(LEVELS):
+                out[q, z] = held[z, slot]
+        for q in quads:
+            send(out.at[q], targets.at[mine], stage, target_sem, on_member(level, q))
+        targets[mine] = out[mine]
+
     def pack(k, arrays):
         for q in range(QUAD):
             for a in range(3):
                 q1_send[k, q, a] = arrays[a][:, q * part : (q + 1) * part]
-        for q in quads:
-            send(q1_send.at[k, q], q1_recv.at[k, mine], 3, q1_sem.at[k], on_member(level, q))
-        q1_recv[k, mine] = q1_send[k, mine]
-
-    def spread(k):
-        await_bytes(q1_recv.at[k, pl.ds(0, QUAD - 1)], q1_sem.at[k])
-        q1_held[...] = q1_recv[k]
-        for j in range(win_slots):
-            chosen = q1_held[table[level * QUAD + j]]
-            for z in range(LEVELS):
-                z1_send[k, z, j] = chosen[:, z * 16 : (z + 1) * 16, :]
-        for z in levels:
-            send(z1_send.at[k, z], z1_recv.at[k, level], 4, z1_sem.at[k], on_member(z, mine))
-        z1_recv[k, level] = z1_send[k, level]
+        split(q1_send.at[k], q1_recv.at[k], q1_sem.at[k], c1_recv.at[k], c1_sem.at[k], 3)
+
+    def cross_state(k):
+        cross(
+            q1_send.at[k],
+            c1_recv.at[k],
+            c1_sem.at[k],
+            x1_send.at[k],
+            q1_recv.at[k],
+            q1_sem.at[k],
+            q1_held,
+            10,
+        )
+
+    def select_state(k):
+        select(q1_recv.at[k], q1_sem.at[k], q1_held, z1_send.at[k], 4, z1_recv.at[k], z1_sem.at[k])
+
+    def forward_state(k):
+        forward(z1_recv.at[k], z1_sem.at[k], z1_held, z2_send.at[k], 5, z2_recv.at[k], z2_sem.at[k])
+
+    def deliver_state(k):
+        deliver(z2_recv.at[k], z2_sem.at[k], z2_held, q2_send.at[k], 6, q2_recv.at[k], q2_sem.at[k])
+
+    def cross_gradient(e):
+        cross(
+            g1_send.at[e],
+            c2_recv.at[e],
+            c2_sem.at[e],
+            x2_send.at[e],
+            g1_recv.at[e],
+            g1_sem.at[e],
+            g1_held,
+            11,
+        )
+
+    def select_gradient(e):
+        select(g1_recv.at[e], g1_sem.at[e], g1_held, g2_send.at[e], 7, g2_recv.at[e], g2_sem.at[e])
+
+    def forward_gradient(e):
+        forward(g2_recv.at[e], g2_sem.at[e], g2_held, g3_send.at[e], 8, g3_recv.at[e], g3_sem.at[e])
+
+    def deliver_gradient(e):
+        deliver(g3_recv.at[e], g3_sem.at[e], g3_held, g4_send.at[e], 9, g4_recv.at[e], g4_sem.at[e])
+
+    def either(k, state, gradient):
+        @pl.when(k < plain)
+        def _():
+            state(k)
+
+        @pl.when(k >= plain)
+        def _():
+            gradient(k - plain)
 
     def stage_p(k):
         @pl.when(k == plain)
@@ -288,87 +398,52 @@
             e = k - plain
             for q in range(QUAD):
                 g1_send[e, q] = gradient[:, q * part : (q + 1) * part].astype(jnp.bfloat16)
-            for q in quads:
-                send(g1_send.at[e, q], g1_recv.at[e, mine], 7, g1_sem.at[e], on_member(level, q))
-            g1_recv[e, mine] = g1_send[e, mine]
+            split(g1_send.at[e], g1_recv.at[e], g1_sem.at[e], c2_recv.at[e], c2_sem.at[e], 12)
+
+    def stage_i(k):
+        either(k, cross_state, cross_gradient)
 
     def stage_e(k):
-        @pl.when(k < plain)
-        def _():
-            spread(k)
-
-        @pl.when(k >= plain)
-        def _():
-            e = k - plain
-            await_bytes(g1_recv.at[e, pl.ds(0, QUAD - 1)], g1_sem.at[e])
-            g1_held[...] = g1_recv[e]
-            for j in range(win_slots):
-                chosen = g1_held[table[level * QUAD + j]]
-                for z in range(LEVELS):
-                    g2_send[e, z, j] = chosen[z * 16 : (z + 1) * 16, :]
-            for z in levels:
-                send(g2_send.at[e, z], g2_recv.at[e, level], 8, g2_sem.at[e], on_member(z, mine))
-            g2_recv[e, level] = g2_send[e, level]
+        either(k, select_state, select_gradient)
 
     def stage_f(k):
-        await_bytes(z1_recv.at[k, pl.ds(0, LEVELS - 1)], z1_sem.at[k])
-        z1_held[...] = z1_recv[k]
-
-        @pl.when(k >= plain)
-        def _():
-            e = k - plain
-            await_bytes(g2_recv.at[e, pl.ds(0, LEVELS - 1)], g2_sem.at[e])
-
-            def step_level(z, carry):
-                for j in range(win_slots):
-                    who = z * QUAD + table[z * QUAD + j]
-                    stepped = adam(
-                        z1_held[z, j, 0].astype(jnp.float32),
-                        z1_held[z, j, 1].astype(jnp.float32),
-                        z1_held[z, j, 2].astype(jnp.float32),
-                        g2_recv[e, z, j].astype(jnp.float32),
-                        jnp.full((1, part), rates[who], jnp.float32),
-                        jnp.full((1, part), decays_one[who], jnp.float32),
-                        jnp.full((1, part), decays_two[who], jnp.float32),
-                    )
-                    for a in range(3):
-                        z1_held[z, j, a] = stepped[a].astype(jnp.bfloat16)
-                return carry
-
-            lax.fori_loop(0, LEVELS, step_level, 0)
-
-        for z in range(LEVELS):
-            for j in range(lose_slots):
-                source = table[32 + z * QUAD + j]
-                z2_send[k, z, j] = z1_held[source // QUAD, lax.rem(source, QUAD)]
-        for z in levels:
-            send(z2_send.at[k, z], z2_recv.at[k, level], 5, z2_sem.at[k], on_member(z, mine))
-        z2_recv[k, level] = z2_send[k, level]
+        either(k, forward_state, forward_gradient)
 
     def stage_g(k):
-        await_bytes(z2_recv.at[k, pl.ds(0, LEVELS - 1)], z2_sem.at[k])
-        z2_held[...] = z2_recv[k]
-        for q in range(QUAD):
-            slot = table[64 + level * QUAD + q]
-            for z in range(LEVELS):
-                q2_send[k, q, z] = z2_held[z, slot]
-        for q in quads:
-            send(q2_send.at[k, q], q2_recv.at[k, mine], 6, q2_sem.at[k], on_member(level, q))
-        q2_recv[k, mine] = q2_send[k, mine]
+        either(k, deliver_state, deliver_gradient)
 
     outs = ((out_weight, weight_out), (out_first, first_out), (out_second, second_out))
 
     def stage_h(k):
         row, col = place(k)
         await_bytes(q2_recv.at[k, pl.ds(0, QUAD - 1)], q2_sem.at[k])
-        taken = jnp.full((1, part), table[96 + member], jnp.int32) != 0
-        for q in range(QUAD):
+        source = table[96 + member]
+        taken = jnp.full((1, part), source, jnp.int32) != member
+
+        def keep_or_take(q, copied):
+            here = (pl.ds(row, ROWS), pl.ds(col + q * part, part))
             for a in range(3):
                 ref = outs[a][0]
-                here = (pl.ds(row, ROWS), pl.ds(col + q * part, part))
-                copied = q2_recv[k, q, :, a].reshape(ROWS, part).astype(jnp.float32)
                 kept = ref[here].astype(jnp.float32)
-                ref[here] = jnp.where(taken, copied, kept).astype(ref.dtype)
+                ref[here] = jnp.where(taken, copied[a], kept).astype(ref.dtype)
+
+        def arrived(q):
+            return [q2_recv[k, q, :, a].reshape(ROWS, part).astype(jnp.float32) for a in range(3)]
+
+        @pl.when(k < plain)
+        def _():
+            for q in range(QUAD):
+                keep_or_take(q, arrived(q))
+
+        @pl.when(k >= plain)
+        def _():
+            e = k - plain
+            await_bytes(g4_recv.at[e, pl.ds(0, QUAD - 1)], g4_sem.at[e])
+            hyper = [jnp.full((1, part), ref[source]) for ref in (rates, decays_one, decays_two)]
+            for q in range(QUAD):
+                gradient = g4_recv[e, q].reshape(ROWS, part).astype(jnp.float32)
+                keep_or_take(q, adam(*arrived(q), gradient, *hyper))
+
         for a in range(3):
             here = (pl.ds(row, ROWS), pl.ds(col, cols))
             pltpu.make_async_copy(outs[a][0].at[here], outs[a][1].at[here], out_sem.at[a]).start()
@@ -382,13 +457,17 @@
         f=stage_f,
         g=stage_g,
         h=stage_h,
+        i=stage_i,
         p=stage_p,
-        r=spread,
+        j=cross_state,
+        r=select_state,
+        s=forward_state,
+        t=deliver_state,
     )
 
     def iteration(i, carry):
         for name in order:
-            lowest = plain if name in "pr" else 0
+            lowest = plain if name in "pjrst" else 0
             k = i - lags[name] + lowest
 
             @pl.when((k >= lowest) & (k < chunks))
@@ -399,25 +478,31 @@
 
     lax.fori_loop(0, chunks + lags["h"], iteration, 0)
 
-    sent = (
-        y1_send,
-        y2_send,
-        x_send,
-        q1_send.at[:, pl.ds(0, QUAD - 1)],
-        z1_send.at[:, pl.ds(0, LEVELS - 1)],
-        z2_send.at[:, pl.ds(0, LEVELS - 1)],
-        q2_send.at[:, pl.ds(0, QUAD - 1)],
-        g1_send.at[:, pl.ds(0, QUAD - 1)],
-        g2_send.at[:, pl.ds(0, LEVELS - 1)],
-    )
-    for stage, ref in enumerate(sent):
+    others, peers = pl.ds(0, 2 if by_chip else QUAD - 1), pl.ds(0, QUAD - 1)
+    away = pl.ds(0, LEVELS - 1)
+    sent = [
+        (0, y1_send),
+        (1, y2_send),
+        (2, x_send),
+        (3, q1_send.at[:, others]),
+        (12, g1_send.at[:, others]),
+        (4, z1_send.at[:, away]),
+        (5, z2_send.at[:, away]),
+        (6, q2_send.at[:, peers]),
+        (7, g2_send.at[:, away]),
+        (8, g3_send.at[:, away]),
+        (9, g4_send.at[:, peers]),
+    ]
+    if by_chip:
+        sent += [(10, x1_send.at[:, pl.ds(0, 1)]), (11, x2_send.at[:, pl.ds(0, 1)])]
+    for stage, ref in sent:
         await_bytes(ref, send_sem.at[stage])
     for a in range(3):
         await_bytes(outs[a][0], out_sem.at[a])
 
 
 def step_call(plan, table, rates, ones, twos, *blocks):
-    win_slots, lose_slots, order, lags = PLANS[plan]
+    win_slots, lose_slots, by_chip, early, order, lags = PLANS[plan]
     tokens, cotangent, weight, first, second = blocks
     rows, width = weight.shape
     cols = width // SPLIT
@@ -434,11 +519,16 @@
     z1 = pltpu.VMEM((chunks, LEVELS, win_slots, 3, ROWS // LEVELS, part), kind)
     z2 = pltpu.VMEM((chunks, LEVELS, lose_slots, 3, ROWS // LEVELS, part), kind)
     q2 = pltpu.VMEM((chunks, QUAD, LEVELS, 3, ROWS // LEVELS, part), kind)
-    g1 = pltpu.VMEM((EARLY, QUAD, ROWS, part), kind)
-    g2 = pltpu.VMEM((EARLY, LEVELS, win_slots, ROWS // LEVELS, part), kind)
+    g1 = pltpu.VMEM((early, QUAD, ROWS, part), kind)
+    g2 = pltpu.VMEM((early, LEVELS, win_slots, ROWS // LEVELS, part), kind)
+    g3 = pltpu.VMEM((early, LEVELS, lose_slots, ROWS // LEVELS, part), kind)
+    g4 = pltpu.VMEM((early, QUAD, LEVELS, ROWS // LEVELS, part), kind)
+    chip = (chunks, early) if by_chip else (1, 1)
+    c1 = pltpu.VMEM((chip[0], 2, 3, ROWS, part), kind)
+    c2 = pltpu.VMEM((chip[1], 2, ROWS, part), kind)
     dma = pltpu.SemaphoreType.DMA
     return pl.pallas_call(
-        functools.partial(step_kernel, win_slots, lose_slots, order, lags),
+        functools.partial(step_kernel, PLANS[plan]),
         out_shape=(
             jax.ShapeDtypeStruct(weight.shape, jnp.float32),
             jax.ShapeDtypeStruct(weight.shape, kind),
@@ -448,16 +538,19 @@
         out_specs=(anywhere,) * 3,
         scratch_shapes=like
         + [like[2], like[3], like[4]]
-        + [y1, y1, y2, y2, beside, beside, q1, q1, z1, z1, z2, z2, q2, q2, g1, g1, g2, g2]
+        + [y1, y1, y2, y2, beside, beside, q1, q1, z1, z1, z2, z2, q2, q2]
+        + [g1, g1, g2, g2, g3, g3, g4, g4, c1, c2, c1, c2]
         + [
             pltpu.VMEM((lags["d"] + 1, 4, ROWS, cols), jnp.float32),
             pltpu.VMEM(q1.shape[1:], kind),
             pltpu.VMEM(z1.shape[1:], kind),
             pltpu.VMEM(z2.shape[1:], kind),
             pltpu.VMEM(g1.shape[1:], kind),
+            pltpu.VMEM(g2.shape[1:], kind),
+            pltpu.VMEM(g3.shape[1:], kind),
             dma((rows // ROWS + 4,)),
             dma((3,)),
-            dma((9,)),
+            dma((13,)),
             dma((chunks, 2)),
             dma((chunks, 2)),
             dma((chunks,)),
@@ -465,8 +558,12 @@
             dma((chunks,)),
             dma((chunks,)),
             dma((chunks,)),
-            dma((EARLY,)),
-            dma((EARLY,)),
+            dma((early,)),
+            dma((early,)),
+            dma((early,)),
+            dma((early,)),
+            dma((chunks,)),
+            dma((early,)),
         ],
         compiler_params=pltpu.CompilerParams(
             collective_id=plan,
@@ -496,28 +593,48 @@
 
     lax.fori_loop(0, members, mark, 0)
 
-    def rank(z, most):
-        wins = losses = jnp.int32(0)
+    def count(z, most):
+        wins = losses = pair = jnp.int32(0)
         for q in range(QUAD):
             m = z * QUAD + q
-            won = winner[m]
-            lost = (sources[m] != m).astype(jnp.int32)
-            place[m] = z * QUAD + wins
-            table[2 * members + m] = jnp.where(lost != 0, losses, 0)
-            table[3 * members + m] = lost
-
-            @pl.when(won != 0)
+            lost = sources[m] != m
+            table[2 * members + m] = jnp.where(lost, losses, 0)
+            table[3 * members + m] = sources[m]
+            wins += winner[m]
+            losses += lost.astype(jnp.int32)
+            if q % 2:
+                pair = jnp.maximum(pair, winner[m - 1] + winner[m])
+        return tuple(jnp.maximum(a, b) for a, b in zip(most, (wins, losses, pair)))
+
+    nothing = (jnp.int32(0),) * 3
+    wins, losses, pair = lax.fori_loop(0, members // QUAD, count, nothing)
+    chosen = jnp.int32(len(PLANS) - 1)
+    for p in reversed(range(len(PLANS))):
+        fits = (wins <= PLANS[p][0]) & (losses <= PLANS[p][1])
+        if PLANS[p][2]:
+            fits &= pair <= 1
+        chosen = jnp.where(fits, p, chosen)
+    plan[0] = chosen
+    by_chip = jnp.bool_(False)
+    for p in range(len(PLANS)):
+        if PLANS[p][2]:
+            by_chip |= chosen == p
+
+    def rank(z, carry):
+        wins = jnp.int32(0)
+        for q in range(QUAD):
+            m = z * QUAD + q
+            slot = z * QUAD + jnp.where(by_chip, q // 2, wins)
+            place[m] = slot
+
+            @pl.when(winner[m] != 0)
             def _():
-                table[z * QUAD + wins] = q
-
-            wins += won
-            losses += lost
-        return jnp.maximum(most[0], wins), jnp.maximum(most[1], losses)
-
-    wins, losses = lax.fori_loop(0, members // QUAD, rank, (jnp.int32(0), jnp.int32(0)))
-    plan[0] = jnp.where(
-        wins > 3, 3, jnp.where(losses > 3, 3, jnp.where(wins > 2, 2, jnp.where(losses > 2, 1, 0)))
-    )
+                table[slot] = jnp.where(by_chip, q % 2, q)
+
+            wins += winner[m]
+        return carry
+
+    lax.fori_loop(0, members // QUAD, rank, 0)
 
     def want(m, carry):
         @pl.when(sources[m] != m)

time: 147 us -> 126 us (0.86)
  Pallas kernels: 145 us -> 124 us
    pallas_call x1, Pallas kernels: 138 us -> 118 us  [step_call(): pl.pallas_call(functools.partial(step_kernel, PLANS[plan]), out_shape=(ja...]
where the time goes in v4:
time: 126 us
  Pallas kernels  124 us (98%)
  between operations  1.48 us (1%)
    pallas_call x1, Pallas kernels, step_call(): pl.pallas_call(functools.partial(step_kernel, PLANS[plan]), out_shape=(ja...  118 us
    pallas_call x1, Pallas kernels, copy_call(): pl.pallas_call(functools.partial(copy_kernel, len(arrays)), out_shape=tup...  3.54 us
    pallas_call x1, Pallas kernels, route_call(): pl.pallas_call(route_kernel, out_shape=(jax.ShapeDtypeStruct((4 * members...  3.02 us

profile of v4, /device:TPU:1, one launch (start us, length us, event | category | flops | bytes accessed | tf_op | source)
XLA Modules:
  0.0 125.9 jit_solution(12181766986136605566)
XLA Ops:
  0.6 3.0 %shard_map.129 = (s32[128]{0:T(128)S(1)}, s32[1]{0:T(128)}, f32[1,32]{1,0:T(1,128)}) custom-call(s32[32]{0:T(128)} %sources.1, f32[32]{0:T(128)} %rates.1, s32[32]{0:T(128)} %perturb.1), custom_call_target="tpu_custom_call" | custom-call | tf_op jit(solution)/shard_map/pallas_call | solution.py:665
  4.3 117.9 %conditional.1 = ((f32[512,1024]{1,0:T(8,128)}, bf16[512,1024]{1,0:T(8,128)(2,1)}, bf16[512,1024]{1,0:T(8,128)(2,1)})) conditional(s32[]{:T(128)} %bitcast, (s32[128]{0:T(128)S(1)}, f32[32]{0:T(128)}, f32[32]{0:T(128)}, f32[32]{0:T(128)}, bf16[512,4096]{1,0:T(8,128)(2,1)}, /*index=5*/bf16[512,1024]{1,0:T(8,128)(2,1)}, ...), branch_computations={%region_0.0_spmd, %region_1.0_spmd, %region_2.0_spmd, %region_3.0_... | conditional | bytes 8 | solution.py:728
  4.3 117.6 %branch_1_fun.1 = (f32[512,1024]{1,0:T(8,128)}, bf16[512,1024]{1,0:T(8,128)(2,1)}, bf16[512,1024]{1,0:T(8,128)(2,1)}) custom-call(s32[128]{0:T(128)S(1)} %get-tuple-element.99.table, f32[32]{0:T(128)} %get-tuple-element.100.rates, f32[32]{0:T(128)} %get-tuple-element.101.decays_one, f32[32]{0:T(128)} %get-tuple-element.102.decays_two, ...), custom_call_target="tpu_custom_call" | custom-call | tf_op jit(solution)/shard_map/cond/branch_1_fun/pallas_call | solution.py:530
  122.2 3.5 %shard_map.130 = (f32[512,1024]{1,0:T(8,128)}, bf16[512,1024]{1,0:T(8,128)(2,1)}, bf16[512,1024]{1,0:T(8,128)(2,1)}) custom-call(f32[512,1024]{1,0:T(8,128)} %get-tuple-element.150.refs_0_, bf16[512,1024]{1,0:T(8,128)(2,1)} %get-tuple-element.151.refs_1_, bf16[512,1024]{1,0:T(8,128)(2,1)} %get-tuple-element.152.refs_2_), custom_call_target="tpu_custom_call" | custom-call | tf_op jit(solution)/shard_map/pallas_call | solution.py:705
